TPU v7x, 512 devices: a whole 4x4x16 slice. The times are simulated.
512 devices in a mesh: dp: 8 (over y_lo, x), pipe: 4 (over y_hi, core), tensor: 16 (over z).
Axes of the slice: x: 4, y: 4 (y_hi: 2, y_lo: 2; y = y_hi * 2 + y_lo), z: 16, core: 2. Of those that a mesh axis runs over, the one named last changes fastest.
Arguments:
- saved_input: bfloat16 [8, 4, 1024, 1536], P('dp', 'pipe', 'tensor'), may hold values from -6 to 6
- grad_in: bfloat16 [8, 4, 1024, 1536], P('dp', 'pipe', 'tensor'), may hold values from -6 to 6
- segment_ids: int32 [8, 4, 1024], P('dp', 'pipe'), may hold values from 0 to 7, never falling along the last dimension, each value on 1 to 256 neighbouring positions
- w_qkv: bfloat16 [4, 1536, 16, 384], P('pipe', 'dp', 'tensor'), may hold values from -0.15625 to 0.15625
- w_out: bfloat16 [4, 16, 128, 1536], P('pipe', 'tensor', 'dp'), may hold values from -0.125 to 0.125
- q_gain: float32 [4, 128], P('pipe'), may hold values from 0.5 to 1.5
- k_gain: float32 [4, 128], P('pipe'), may hold values from 0.5 to 1.5
Outputs:
- grad_out: bfloat16 [8, 4, 1024, 1536], P('dp', 'pipe', 'tensor')
- grad_qkv: bfloat16 [4, 1536, 16, 384], P('pipe', None, 'tensor')
- grad_wout: bfloat16 [4, 16, 128, 1536], P('pipe', 'tensor')
Inputs may be any that keep to these rules, and one draw needn't show every extreme that they name: `segment_ids`: in each micro-batch the ids never fall along the tokens; every id 0 to 7 occurs, on 1 to 256 tokens, and one clip has exactly 256.
All inputs are finite; a program needn't handle non-finite values.
Results may differ from a plain program's by a relative error of at most 0.019.
Values may be sent and summed in bfloat16 or wider, within the bound.
No kernel may reach another device: no remote copies, remote signals or barrier semaphores. Data moves between devices by JAX's collectives and lax.ppermute only.
A program may use at most 64 MiB of HBM per device.

v0:
```python
import jax
import jax.numpy as jnp
from jax import lax
from jax.sharding import PartitionSpec as P

EPS = 1e-06


def from_behind(array, axis, by):
    peers = lax.axis_size(axis)
    return lax.ppermute(array, axis, [(i, (i + by) % peers) for i in range(peers)])


def contract(left, right, left_dim, right_dim):
    return lax.dot_general(
        left, right, (((left_dim,), (right_dim,)), ((), ())), preferred_element_type=jnp.float32
    )


def per_device(saved_input, grad_in, segment_ids, w_qkv, w_out, q_gain, k_gain):
    x_float = saved_input[0, 0].astype(jnp.float32)
    centred = x_float - jnp.mean(x_float, axis=-1, keepdims=True)
    scaled = lax.rsqrt(jnp.mean(centred * centred, axis=-1, keepdims=True) + EPS)
    unit = centred * scaled
    normed_rows = unit.astype(jnp.bfloat16)
    cot_rows = grad_in[0, 0]
    proj_full, outw_full = (
        lax.all_gather(w_qkv[0, :, 0, :], "dp", axis=0, tiled=True),
        lax.all_gather(w_out[0, 0], "dp", axis=0, tiled=True),
    )
    normed, cotangent = (
        lax.all_gather(normed_rows, "tensor", axis=0, tiled=True),
        lax.all_gather(cot_rows, "tensor", axis=0, tiled=True),
    )
    width = outw_full.shape[0]
    factor = width ** (-0.5)
    q_scale = q_gain[0]
    k_scale = k_gain[0]
    segments = segment_ids[0, 0]
    same_segment = (segments[:, None] == segments[None, :]).astype(jnp.float32)
    joined = jnp.dot(normed, proj_full, preferred_element_type=jnp.float32)
    query = joined[:, :width]
    keys = joined[:, width : 2 * width]
    values = joined[:, 2 * width :]
    q_rate = lax.rsqrt(jnp.mean(query * query, axis=-1, keepdims=True) + EPS)
    q_unit = query * q_rate
    q_norm = (q_unit * q_scale).astype(jnp.bfloat16)
    k_rate = lax.rsqrt(jnp.mean(keys * keys, axis=-1, keepdims=True) + EPS)
    k_unit = keys * k_rate
    k_norm = (k_unit * k_scale).astype(jnp.bfloat16)
    v_low = values.astype(jnp.bfloat16)
    scores = contract(q_norm, k_norm, 1, 1) * factor
    expd = jnp.exp(scores) * same_segment
    probs = expd / jnp.sum(expd, axis=-1, keepdims=True)
    probs_low = probs.astype(jnp.bfloat16)
    attended = jnp.dot(probs_low, v_low, preferred_element_type=jnp.float32).astype(jnp.bfloat16)
    d_attended = contract(cotangent, outw_full, 1, 1).astype(jnp.bfloat16)
    d_outw = contract(attended, cotangent, 0, 0)
    d_probs = contract(d_attended, v_low, 1, 1)
    d_values = contract(probs_low, d_attended, 0, 0)
    row_delta = jnp.sum(probs * d_probs, axis=-1, keepdims=True)
    d_scores = (probs * (d_probs - row_delta) * factor).astype(jnp.bfloat16)
    d_qnorm = jnp.dot(d_scores, k_norm, preferred_element_type=jnp.float32)
    d_knorm = contract(d_scores, q_norm, 0, 0)
    q_back = d_qnorm * q_scale
    d_query = q_rate * (q_back - q_unit * jnp.mean(q_back * q_unit, axis=-1, keepdims=True))
    k_back = d_knorm * k_scale
    d_keys = k_rate * (k_back - k_unit * jnp.mean(k_back * k_unit, axis=-1, keepdims=True))
    d_joined = jnp.concatenate([d_query, d_keys, d_values], axis=-1).astype(jnp.bfloat16)
    d_proj = contract(normed, d_joined, 0, 0)
    proj_sum, out_sum = (
        lax.psum(d_proj.astype(jnp.bfloat16), "dp").astype(jnp.float32),
        lax.psum(d_outw.astype(jnp.bfloat16), "dp").astype(jnp.float32),
    )
    d_normed = lax.psum_scatter(
        contract(d_joined, proj_full, 1, 1).astype(jnp.bfloat16),
        "tensor",
        scatter_dimension=0,
        tiled=True,
    ).astype(jnp.float32)
    d_tokens = cot_rows.astype(jnp.float32) + scaled * (
        d_normed
        - jnp.mean(d_normed, axis=-1, keepdims=True)
        - unit * jnp.mean(d_normed * unit, axis=-1, keepdims=True)
    )
    passed = from_behind(d_tokens.astype(jnp.bfloat16), "pipe", -1)
    return (
        passed[None, None],
        proj_sum.astype(jnp.bfloat16)[None, :, None, :],
        out_sum.astype(jnp.bfloat16)[None, None],
    )


def solution(mesh):
    placed = (
        P("dp", "pipe", "tensor", None),
        P("dp", "pipe", "tensor", None),
        P("dp", "pipe", None),
        P("pipe", "dp", "tensor", None),
        P("pipe", "tensor", "dp", None),
        P("pipe", None),
        P("pipe", None),
    )
    return jax.shard_map(
        per_device,
        mesh=mesh,
        in_specs=placed,
        out_specs=(
            P("dp", "pipe", "tensor", None),
            P("pipe", None, "tensor", None),
            P("pipe", "tensor", None, None),
        ),
        check_vma=False,
    )
```

profile of v0, /device:TPU:1, one launch (start us, length us, event | category | flops | bytes accessed | tf_op | source)
XLA Modules:
  0.0 406.9 jit_solution(17134687508166921309)
XLA Ops:
  7.2 0.7 all-gather.9.cloned.1.call-update
  7.9 1.1 convert_reduce_fusion.1
  9.0 1.2 fusion.32
  10.2 1.7 fusion.27
  12.0 0.7 all-gather.11.cloned.1.call-update
  12.7 24.4 %all-gather.2 = bf16[1,1,128,1536]{3,2,1,0:T(8,128)(2,1)S(1)} all-gather(bf16[1,1,16,1536]{3,2,1,0:T(8,128)(2,1)} %param.11), channel_id=4, replica_groups=mesh['dp'=8,'pipe'=4,'tensor'=16] {'dp'}, dimensions={2}, use_global_device_ids=true | all-gather | bytes 442368 | tf_op jit(solution)/shard_map/all_gather | solution.py:29
  37.1 21.0 %all-gather.9.cloned.1.call-done = bf16[1,1536,1,384]{3,1,2,0:T(8,128)(2,1)} async-done(((bf16[1,192,1,384]{3,1,2,0:T(8,128)(2,1)}), bf16[1,1536,1,384]{3,1,2,0:T(8,128)(2,1)}) %all-gather.9.cloned.1.call-update) | async-done | bytes 1179664 | tf_op jit(solution)/shard_map/all_gather | solution.py:28
  58.1 74.2 %all-gather.7.cloned.1.call-done = bf16[1024,1536]{1,0:T(8,128)(2,1)} async-done(((bf16[64,1536]{1,0:T(8,128)(2,1)}), bf16[1024,1536]{1,0:T(8,128)(2,1)}) %all-gather.7.cloned.1.call-update) | async-done | bytes 3145744 | tf_op jit(solution)/shard_map/all_gather | solution.py:32
  132.3 3.6 fusion.17
  136.1 3.0 fusion.1
  139.1 68.6 %all-gather.11.cloned.1.call-done = bf16[1,1,1024,1536]{3,2,1,0:T(8,128)(2,1)} async-done(((bf16[1,1,64,1536]{3,2,1,0:T(8,128)(2,1)}), bf16[1,1,1024,1536]{3,2,1,0:T(8,128)(2,1)}) %all-gather.11.cloned.1.call-update) | async-done | bytes 3145744 | tf_op jit(solution)/shard_map/all_gather | solution.py:33
  207.7 3.0 fusion.13
  210.8 1.7 convolution_convert_fusion.3
  212.5 1.4 multiply_reduce_fusion
  213.9 1.7 multiply_convert_fusion
  215.7 0.8 convolution_multiply_fusion.1
  216.6 0.7 multiply_reduce_fusion.2
  217.3 0.3 multiply_convert_fusion.2
  217.5 0.3 copy-done.6
  217.8 3.5 convolution_convert_fusion
  221.4 0.2 all-reduce.3.cloned.1.call-start
  221.6 4.8 %fusion.6 = bf16[1,1536,1,384]{3,1,2,0:T(8,128)(2,1)} fusion(bf16[1024,1536]{1,0:T(8,128)(2,1)} %all-gather.7.cloned.1.call-done, bf16[1024,128]{0,1:T(8,128)(2,1)S(1)} %convolution_convert_fusion.3, bf16[1024,128]{0,1:T(8,128)(2,1)S(1)} %get-tuple-element.12, bf16[1024,128]{0,1:T(8,128)(2,1)S(1)} %get-tuple-element.11), kind=kOutput, calls=%fused_computation.11 | convolution fusion | flops 1210908672 | bytes 5111808 | tf_op jit(solution)/shard_map/dot_general | solution.py:15
  226.4 6.1 %fusion.10 = bf16[1,1,128,1536]{3,2,1,0:T(8,128)(2,1)} fusion(bf16[1,1,1024,1536]{3,2,1,0:T(8,128)(2,1)} %all-gather.11.cloned.1.call-done, f32[1024,384]{0,1:T(8,128)S(1)} %fusion.17, f32[1024,1024]{0,1:T(8,128)} %get-tuple-element.14, f32[1024]{0:T(1024)S(1)} %get-tuple-element.13, s32[1024]{0:T(1024)S(1)} %bitcast.67), kind=kOutput, calls=%fused_computation.13 | convolution fusion | flops 676659200 | bytes 8007680 | tf_op jit(solution)/shard_map/dot_general | solution.py:15
  232.5 62.1 %reduce-scatter.2.cloned.1.call-done = bf16[64,1536]{1,0:T(8,128)(2,1)} async-done(((bf16[1024,1536]{1,0:T(8,128)(2,1)}), bf16[64,1536]{1,0:T(8,128)(2,1)}) %reduce-scatter.2.cloned.1.call-update) | async-done | bytes 196624 | tf_op jit(solution)/shard_map/reduce_scatter | solution.py:75
  294.6 1.2 convert_reduce_fusion
  295.9 1.1 fusion.31
  297.0 11.8 %collective-permute-start = (bf16[64,1536]{1,0:T(8,128)(2,1)S(1)}, bf16[64,1536]{1,0:T(8,128)(2,1)S(1)}, u32[]{:S(2)}, u32[]{:S(2)}) collective-permute-start(bf16[64,1536]{1,0:T(8,128)(2,1)S(1)} %fusion.31), channel_id=1, source_target_pairs={{0,48},{16,0},{32,16},{48,32},{1,49},{17,1},{33,17},{49,33},{2,50}... | collective-permute-start | bytes 589832 | tf_op jit(solution)/shard_map/ppermute | solution.py:11
  308.8 6.2 %collective-permute-done = bf16[64,1536]{1,0:T(8,128)(2,1)S(1)} collective-permute-done((bf16[64,1536]{1,0:T(8,128)(2,1)S(1)}, bf16[64,1536]{1,0:T(8,128)(2,1)S(1)}, u32[]{:S(2)}, u32[]{:S(2)}) %collective-permute-start) | collective-permute-done | bytes 196640 | tf_op jit(solution)/shard_map/ppermute | solution.py:11
  315.0 80.5 %all-reduce.3.cloned.1.call-done = (bf16[1,1536,1,384]{3,1,2,0:T(8,128)(2,1)}, bf16[1,1,128,1536]{3,2,1,0:T(8,128)(2,1)}) async-done(((bf16[1,1536,1,384]{3,1,2,0:T(8,128)(2,1)}, bf16[1,1,128,1536]{3,2,1,0:T(8,128)(2,1)}), (bf16[1,1536,1,384]{3,1,2,0:T(8,128)(2,1)}, bf16[1,1,128,1536]{3,2,1,0:T(8,128)(2,1)})) %all-reduce.3.cloned.1.call-update) | async-done | bytes 1572880 | tf_op jit(solution)/shard_map/psum | solution.py:72
  395.5 0.7 copy.13
  396.2 2.4 copy.14
  398.6 1.8 copy.15
  (28 shorter events, 0.5 us)
Async XLA Ops:
  7.2 50.9 %all-gather.9.cloned.1.call-start = ((), (), s32[]{:S(2)}) async-start(), calls=%async_computation.3 | async-start | bytes 1327104 | tf_op jit(solution)/shard_map/all_gather | solution.py:28
  7.9 124.4 %all-gather.7.cloned.1.call-start = ((), (), s32[]{:S(2)}) async-start(), calls=%async_computation.1 | async-start | bytes 3342336 | tf_op jit(solution)/shard_map/all_gather | solution.py:32
  11.9 195.7 %all-gather.11.cloned.1.call-start = ((), (), s32[]{:S(2)}) async-start(), calls=%async_computation.4 | async-start | bytes 3342336 | tf_op jit(solution)/shard_map/all_gather | solution.py:33
  12.7 281.9 %reduce-scatter.2.cloned.1.call-start = ((), (), s32[]{:S(2)}) async-start(), calls=%async_computation.2 | async-start | bytes 3342336 | tf_op jit(solution)/shard_map/reduce_scatter | solution.py:75
  37.1 99.0 %copy-start.3 = (s32[1,1,1024]{2,1,0:T(1,128)S(1)}, s32[1,1,1024]{2,1,0:T(1,128)}, u32[]{:S(2)}) copy-start(s32[1,1,1024]{2,1,0:T(1,128)} %param.9) | copy-start | bytes 12292
  37.1 99.0 %copy-start.4 = (f32[1,128]{1,0:T(1,128)S(1)}, f32[1,128]{1,0:T(1,128)}, u32[]{:S(2)}) copy-start(f32[1,128]{1,0:T(1,128)} %param.13) | copy-start | bytes 1540
  37.1 99.0 %copy-start.5 = (f32[1,128]{1,0:T(1,128)S(1)}, f32[1,128]{1,0:T(1,128)}, u32[]{:S(2)}) copy-start(f32[1,128]{1,0:T(1,128)} %param.12) | copy-start | bytes 1540
  207.7 3.1 copy-start.1
  216.6 1.3 copy-start.6
  221.4 174.1 %all-reduce.3.cloned.1.call-start = ((), (), s32[]{:S(2)}) async-start(), calls=%async_computation.5 | async-start | bytes 3145728 | tf_op jit(solution)/shard_map/psum | solution.py:72
  226.4 68.3 %copy-start = (bf16[1,1,64,1536]{3,2,1,0:T(8,128)(2,1)S(1)}, bf16[1,1,64,1536]{3,2,1,0:T(8,128)(2,1)}, u32[]{:S(2)}) copy-start(bf16[1,1,64,1536]{3,2,1,0:T(8,128)(2,1)} %param.7) | copy-start | bytes 589828
  226.4 69.5 %copy-start.2 = (bf16[1,1,64,1536]{3,2,1,0:T(8,128)(2,1)S(1)}, bf16[1,1,64,1536]{3,2,1,0:T(8,128)(2,1)}, u32[]{:S(2)}) copy-start(bf16[1,1,64,1536]{3,2,1,0:T(8,128)(2,1)} %param.8) | copy-start | bytes 589828
  297.0 18.0 %collective-permute-start = (bf16[64,1536]{1,0:T(8,128)(2,1)S(1)}, bf16[64,1536]{1,0:T(8,128)(2,1)S(1)}, u32[]{:S(2)}, u32[]{:S(2)}) collective-permute-start(bf16[64,1536]{1,0:T(8,128)(2,1)S(1)} %fusion.31), channel_id=1, source_target_pairs={{0,48},{16,0},{32,16},{48,32},{1,49},{17,1},{33,17},{49,33},{2,50}... | collective-permute-start | bytes 589832 | tf_op jit(solution)/shard_map/ppermute | solution.py:11
Sparse Core Ops, SparseCore 0:
  10.1 47.9 all-gather.8
  60.7 71.5 all-gather.6
  134.4 73.2 all-gather.10
  221.5 73.0 reduce-scatter.1
  298.1 97.4 all-reduce.2
where the time goes:
time: 410 us; the launch traced here: 407 us
  waiting for transfers between devices  314 us (77%)
  matrix products  28.7 us (7%)
  blocking collectives  24.4 us (6%)
  between operations  14 us (3%)
  starting transfers between devices  12.2 us (3%)
  other arithmetic  8.41 us (2%)
  local copies, waits for them, and re-layouts  5.29 us (1%)
    psum x1, waiting for transfers between devices, per_device(): lax.psum(d_proj.astype(jnp.bfloat16), 'dp').astype(jnp.float32)  80.5 us
    all_gather x1, waiting for transfers between devices, per_device(): lax.all_gather(normed_rows, 'tensor', axis=0, tiled=True)  74.2 us
    all_gather x1, waiting for transfers between devices, per_device(): lax.all_gather(cot_rows, 'tensor', axis=0, tiled=True)  68.6 us
    reduce_scatter x1, waiting for transfers between devices, per_device(): lax.psum_scatter(contract(d_joined, proj_full, 1, 1).astype(jnp.bfloat16)...  62.1 us
    dot_general x8, matrix products, contract(): lax.dot_general(left, right, (((left_dim,), (right_dim,)), ((), ())), pre...  24.4 us
    all_gather x1, blocking collectives, per_device(): lax.all_gather(w_out[0, 0], 'dp', axis=0, tiled=True)  24.4 us
    all_gather x1, waiting for transfers between devices, per_device(): lax.all_gather(w_qkv[0, :, 0, :], 'dp', axis=0, tiled=True)  21 us
    ppermute x1, starting transfers between devices, from_behind(): lax.ppermute(array, axis, [(i, (i + by) % peers) for i in range(peers)])  11.8 us
  transfers between devices with their start and end apart: 6, of which 6 were waited for; matrix products, arithmetic and copies ran while one was open for 6% of the time, Pallas kernels for 0%

commit v1 on v0

--- a/solution.py
+++ b/solution.py
@@ -6,7 +6,7 @@
 EPS = 1e-06
 
 
-def from_behind(array, axis, by):
+def shifted(array, axis, by):
     peers = lax.axis_size(axis)
     return lax.ppermute(array, axis, [(i, (i + by) % peers) for i in range(peers)])
 
@@ -17,26 +17,57 @@
     )
 
 
+def ring_gather(block, axis):
+    peers = lax.axis_size(axis)
+    got = {0: block}
+    up = down = block
+    for step in range(1, peers // 2 + 1):
+        up = shifted(up, axis, 1)
+        got[peers - step] = up
+        if step < peers - step:
+            down = shifted(down, axis, -1)
+            got[step] = down
+    return [got[i] for i in range(peers)]
+
+
+def fold_wide(wide, parts, width):
+    rows, cols = wide.shape
+    cut = [wide[:, c : c + width].reshape(parts, rows // parts, width) for c in range(0, cols, width)]
+    return jnp.concatenate(cut, axis=1)
+
+
+def unfold_wide(folded, cols):
+    parts, rows, width = folded.shape
+    high = rows * width // cols
+    cut = [folded[:, i * high : (i + 1) * high].reshape(parts * high, width) for i in range(cols // width)]
+    return jnp.concatenate(cut, axis=1)
+
+
 def per_device(saved_input, grad_in, segment_ids, w_qkv, w_out, q_gain, k_gain):
+    dp = lax.axis_size("dp")
+    me = lax.axis_index("tensor")
     x_float = saved_input[0, 0].astype(jnp.float32)
+    rows = x_float.shape[0]
     centred = x_float - jnp.mean(x_float, axis=-1, keepdims=True)
     scaled = lax.rsqrt(jnp.mean(centred * centred, axis=-1, keepdims=True) + EPS)
     unit = centred * scaled
-    normed_rows = unit.astype(jnp.bfloat16)
     cot_rows = grad_in[0, 0]
-    proj_full, outw_full = (
-        lax.all_gather(w_qkv[0, :, 0, :], "dp", axis=0, tiled=True),
-        lax.all_gather(w_out[0, 0], "dp", axis=0, tiled=True),
-    )
-    normed, cotangent = (
-        lax.all_gather(normed_rows, "tensor", axis=0, tiled=True),
-        lax.all_gather(cot_rows, "tensor", axis=0, tiled=True),
-    )
+    three = w_qkv.shape[3]
+    share = w_qkv.shape[1]
+    weights = jnp.concatenate([w_qkv[0, :, 0, :], fold_wide(w_out[0, 0], 1, three)[0]], axis=0)
+    weights = lax.all_gather(weights, "dp", axis=0)
+    proj_full = weights[:, :share].reshape(dp * share, three)
+    outw_full = unfold_wide(weights[:, share:], w_out.shape[3])
+    blocks = ring_gather(jnp.concatenate([unit.astype(jnp.bfloat16), cot_rows], axis=0), "tensor")
+    normed = jnp.concatenate([b[:rows] for b in blocks], axis=0)
+    cotangent = jnp.concatenate([b[rows:] for b in blocks], axis=0)
+    tokens = normed.shape[0]
     width = outw_full.shape[0]
     factor = width ** (-0.5)
     q_scale = q_gain[0]
     k_scale = k_gain[0]
     segments = segment_ids[0, 0]
+    segments = lax.dynamic_slice(jnp.concatenate([segments, segments]), (me * rows,), (tokens,))
     same_segment = (segments[:, None] == segments[None, :]).astype(jnp.float32)
     joined = jnp.dot(normed, proj_full, preferred_element_type=jnp.float32)
     query = joined[:, :width]
@@ -67,28 +98,27 @@
     k_back = d_knorm * k_scale
     d_keys = k_rate * (k_back - k_unit * jnp.mean(k_back * k_unit, axis=-1, keepdims=True))
     d_joined = jnp.concatenate([d_query, d_keys, d_values], axis=-1).astype(jnp.bfloat16)
-    d_proj = contract(normed, d_joined, 0, 0)
-    proj_sum, out_sum = (
-        lax.psum(d_proj.astype(jnp.bfloat16), "dp").astype(jnp.float32),
-        lax.psum(d_outw.astype(jnp.bfloat16), "dp").astype(jnp.float32),
+    in_order = lax.dynamic_slice(
+        jnp.concatenate([d_joined, d_joined], axis=0), (tokens - me * rows, 0), d_joined.shape
     )
-    d_normed = lax.psum_scatter(
-        contract(d_joined, proj_full, 1, 1).astype(jnp.bfloat16),
-        "tensor",
-        scatter_dimension=0,
-        tiled=True,
-    ).astype(jnp.float32)
+    term = contract(in_order, proj_full, 1, 1).astype(jnp.bfloat16)
+    d_normed = lax.psum_scatter(term, "tensor", scatter_dimension=0, tiled=True).astype(jnp.float32)
+    d_proj = contract(normed, d_joined, 0, 0).astype(jnp.bfloat16)
+    sent = jnp.concatenate(
+        [d_proj.reshape(dp, share, three), fold_wide(d_outw.astype(jnp.bfloat16), dp, three)], axis=1
+    )
+    terms = lax.all_to_all(sent, "dp", 0, 0)
+    total = jnp.sum(terms.astype(jnp.float32), axis=0).astype(jnp.bfloat16)
+    sums = lax.all_to_all(jnp.broadcast_to(total[None], terms.shape), "dp", 0, 0)
+    grad_qkv = sums[:, :share].reshape(dp * share, three)
+    grad_wout = unfold_wide(sums[:, share:], w_out.shape[3])
     d_tokens = cot_rows.astype(jnp.float32) + scaled * (
         d_normed
         - jnp.mean(d_normed, axis=-1, keepdims=True)
         - unit * jnp.mean(d_normed * unit, axis=-1, keepdims=True)
     )
-    passed = from_behind(d_tokens.astype(jnp.bfloat16), "pipe", -1)
-    return (
-        passed[None, None],
-        proj_sum.astype(jnp.bfloat16)[None, :, None, :],
-        out_sum.astype(jnp.bfloat16)[None, None],
-    )
+    passed = shifted(d_tokens.astype(jnp.bfloat16), "pipe", -1)
+    return passed[None, None], grad_qkv[None, :, None, :], grad_wout[None, None]
 
 
 def solution(mesh):

time: 410 us -> 239 us (0.58)
  waiting for transfers between devices: 314 us -> 58.1 us
  starting transfers between devices: 12.2 us -> 70.3 us
  local copies, waits for them, and re-layouts: 5.29 us -> 18.8 us
  blocking collectives: 24.4 us -> 35.9 us
  other arithmetic: 8.41 us -> 13 us
    all_gather x3 -> x1, waiting for transfers between devices: 164 us -> 0.01 us  [per_device(): weights = lax.all_gather(weights, 'dp', axis=0)]
    psum x1 -> x0, waiting for transfers between devices: 80.5 us -> none  [per_device(): lax.psum(d_proj.astype(jnp.bfloat16), 'dp').astype(jnp.float32)]
    ppermute x1 -> x16, starting transfers between devices: 11.8 us -> 70.2 us  [shifted(): lax.ppermute(array, axis, [(i, (i + by) % peers) for i in range(peers)])]
    reduce_scatter x1, waiting for transfers between devices: 62.1 us -> 24.7 us  [per_device(): lax.psum_scatter(term, 'tensor', scatter_dimension=0, tiled=True)]
    all_to_all x0 -> x2, blocking collectives: none -> 35.9 us  [the longest x1 18.2 us: per_device(): terms = lax.all_to_all(sent, 'dp', 0, 0)]
    ppermute x1 -> x16, waiting for transfers between devices: 6.2 us -> 33.4 us  [shifted(): lax.ppermute(array, axis, [(i, (i + by) % peers) for i in range(peers)])]
    all_gather x1 -> x0, blocking collectives: 24.4 us -> none  [per_device(): lax.all_gather(w_out[0, 0], 'dp', axis=0, tiled=True)]
    unnamed x17 -> x34, local copies, waits for them, and re-layouts: 5.29 us -> 13.3 us
  transfers between devices with their start and end apart: 6 -> 18, of which waited for: 6 -> 10; matrix products, arithmetic and copies ran while one was open for 6% -> 10% of each run, Pallas kernels for 0% -> 0%
where the time goes in v1:
time: 239 us; the launch traced here: 238 us
  starting transfers between devices  70.3 us (29%)
  waiting for transfers between devices  58.1 us (24%)
  blocking collectives  35.9 us (15%)
  matrix products  27.8 us (12%)
  local copies, waits for them, and re-layouts  18.8 us (8%)
  between operations  14.5 us (6%)
  other arithmetic  13 us (5%)
    ppermute x16, starting transfers between devices, shifted(): lax.ppermute(array, axis, [(i, (i + by) % peers) for i in range(peers)])  70.2 us
    ppermute x16, waiting for transfers between devices, shifted(): lax.ppermute(array, axis, [(i, (i + by) % peers) for i in range(peers)])  33.4 us
    dot_general x8, matrix products, contract(): lax.dot_general(left, right, (((left_dim,), (right_dim,)), ((), ())), pre...  25.9 us
    reduce_scatter x1, waiting for transfers between devices, per_device(): lax.psum_scatter(term, 'tensor', scatter_dimension=0, tiled=True)  24.7 us
    all_to_all x1, blocking collectives, per_device(): terms = lax.all_to_all(sent, 'dp', 0, 0)  18.2 us
    all_to_all x1, blocking collectives, per_device(): lax.all_to_all(jnp.broadcast_to(total[None], terms.shape), 'dp', 0, 0)  17.7 us
    unnamed x34, local copies, waits for them, and re-layouts  13.3 us
  transfers between devices with their start and end apart: 18, of which 10 were waited for; matrix products, arithmetic and copies ran while one was open for 10% of the time, Pallas kernels for 0%

profile of v1, /device:TPU:1, one launch (start us, length us, event | category | flops | bytes accessed | tf_op | source)
XLA Modules:
  0.0 238.3 jit_solution(14139164166687011858)
XLA Ops:
  12.1 12.0 %collective-permute-start = (bf16[128,1536]{1,0:T(8,128)(2,1)S(1)}, bf16[128,1536]{1,0:T(8,128)(2,1)S(1)}, u32[]{:S(2)}, u32[]{:S(2)}) collective-permute-start(bf16[128,1536]{1,0:T(8,128)(2,1)S(1)} %pad_maximum_fusion), channel_id=1, source_target_pairs={{0,15},{1,0},{2,1},{3,2},{4,3},{5,4},{6,5},{7,6},{8,7},{9,8},{10,9... | collective-permute-start | bytes 1179656 | tf_op jit(solution)/shard_map/ppermute | solution.py:11
  24.1 1.9 collective-permute-start.7
  31.8 5.3 %collective-permute-start.1 = (bf16[128,1536]{1,0:T(8,128)(2,1)S(1)}, bf16[128,1536]{1,0:T(8,128)(2,1)S(1)}, u32[]{:S(2)}, u32[]{:S(2)}) collective-permute-start(bf16[128,1536]{1,0:T(8,128)(2,1)S(1)} %collective-permute-done), channel_id=1, source_target_pairs={{0,15},{1,0},{2,1},{3,2},{4,3},{5,4},{6,5},{7,6},{8,7},{9,8},{10,9... | collective-permute-start | bytes 1179656 | tf_op jit(solution)/shard_map/ppermute | solution.py:11
  37.2 1.9 collective-permute-start.8
  39.9 4.1 %collective-permute-done.1 = bf16[128,1536]{1,0:T(8,128)(2,1)S(1)} collective-permute-done((bf16[128,1536]{1,0:T(8,128)(2,1)S(1)}, bf16[128,1536]{1,0:T(8,128)(2,1)S(1)}, u32[]{:S(2)}, u32[]{:S(2)}) %collective-permute-start.1) | collective-permute-done | bytes 393248 | tf_op jit(solution)/shard_map/ppermute | solution.py:11
  44.0 5.3 %collective-permute-start.2 = (bf16[128,1536]{1,0:T(8,128)(2,1)S(1)}, bf16[128,1536]{1,0:T(8,128)(2,1)S(1)}, u32[]{:S(2)}, u32[]{:S(2)}) collective-permute-start(bf16[128,1536]{1,0:T(8,128)(2,1)S(1)} %collective-permute-done.1), channel_id=1, source_target_pairs={{0,15},{1,0},{2,1},{3,2},{4,3},{5,4},{6,5},{7,6},{8,7},{9,8},{10,9... | collective-permute-start | bytes 1179656 | tf_op jit(solution)/shard_map/ppermute | solution.py:11
  49.3 1.9 collective-permute-start.9
  52.0 3.2 %collective-permute-done.2 = bf16[128,1536]{1,0:T(8,128)(2,1)S(1)} collective-permute-done((bf16[128,1536]{1,0:T(8,128)(2,1)S(1)}, bf16[128,1536]{1,0:T(8,128)(2,1)S(1)}, u32[]{:S(2)}, u32[]{:S(2)}) %collective-permute-start.2) | collective-permute-done | bytes 393248 | tf_op jit(solution)/shard_map/ppermute | solution.py:11
  55.2 5.3 %collective-permute-start.3 = (bf16[128,1536]{1,0:T(8,128)(2,1)S(1)}, bf16[128,1536]{1,0:T(8,128)(2,1)S(1)}, u32[]{:S(2)}, u32[]{:S(2)}) collective-permute-start(bf16[128,1536]{1,0:T(8,128)(2,1)S(1)} %collective-permute-done.2), channel_id=1, source_target_pairs={{0,15},{1,0},{2,1},{3,2},{4,3},{5,4},{6,5},{7,6},{8,7},{9,8},{10,9... | collective-permute-start | bytes 1179656 | tf_op jit(solution)/shard_map/ppermute | solution.py:11
  60.6 1.9 collective-permute-start.10
  63.3 2.2 collective-permute-done.3
  65.5 5.4 %collective-permute-start.4 = (bf16[128,1536]{1,0:T(8,128)(2,1)S(1)}, bf16[128,1536]{1,0:T(8,128)(2,1)S(1)}, u32[]{:S(2)}, u32[]{:S(2)}) collective-permute-start(bf16[128,1536]{1,0:T(8,128)(2,1)S(1)} %collective-permute-done.3), channel_id=1, source_target_pairs={{0,15},{1,0},{2,1},{3,2},{4,3},{5,4},{6,5},{7,6},{8,7},{9,8},{10,9... | collective-permute-start | bytes 1179656 | tf_op jit(solution)/shard_map/ppermute | solution.py:11
  71.0 1.9 collective-permute-start.11
  73.7 2.0 collective-permute-done.4
  75.7 5.0 %collective-permute-start.5 = (bf16[128,1536]{1,0:T(8,128)(2,1)S(1)}, bf16[128,1536]{1,0:T(8,128)(2,1)S(1)}, u32[]{:S(2)}, u32[]{:S(2)}) collective-permute-start(bf16[128,1536]{1,0:T(8,128)(2,1)S(1)} %collective-permute-done.4), channel_id=1, source_target_pairs={{0,15},{1,0},{2,1},{3,2},{4,3},{5,4},{6,5},{7,6},{8,7},{9,8},{10,9... | collective-permute-start | bytes 1179656 | tf_op jit(solution)/shard_map/ppermute | solution.py:11
  80.7 1.9 collective-permute-start.12
  83.4 2.0 collective-permute-done.5
  85.4 5.0 %collective-permute-start.6 = (bf16[128,1536]{1,0:T(8,128)(2,1)S(1)}, bf16[128,1536]{1,0:T(8,128)(2,1)S(1)}, u32[]{:S(2)}, u32[]{:S(2)}) collective-permute-start(bf16[128,1536]{1,0:T(8,128)(2,1)S(1)} %collective-permute-done.5), channel_id=1, source_target_pairs={{0,15},{1,0},{2,1},{3,2},{4,3},{5,4},{6,5},{7,6},{8,7},{9,8},{10,9... | collective-permute-start | bytes 1179656 | tf_op jit(solution)/shard_map/ppermute | solution.py:11
  90.4 1.9 collective-permute-start.13
  94.7 6.0 %collective-permute-done.13 = bf16[128,1536]{1,0:T(8,128)(2,1)S(1)} collective-permute-done((bf16[128,1536]{1,0:T(8,128)(2,1)S(1)}, bf16[128,1536]{1,0:T(8,128)(2,1)S(1)}, u32[]{:S(2)}, u32[]{:S(2)}) %collective-permute-start.13) | collective-permute-done | bytes 393248 | tf_op jit(solution)/shard_map/ppermute | solution.py:11
  100.7 1.9 collective-permute-start.14
  104.5 7.6 %collective-permute-done.14 = bf16[128,1536]{1,0:T(8,128)(2,1)S(1)} collective-permute-done((bf16[128,1536]{1,0:T(8,128)(2,1)S(1)}, bf16[128,1536]{1,0:T(8,128)(2,1)S(1)}, u32[]{:S(2)}, u32[]{:S(2)}) %collective-permute-start.14) | collective-permute-done | bytes 393248 | tf_op jit(solution)/shard_map/ppermute | solution.py:11
  120.9 4.4 %convolution_convert_fusion.5 = bf16[1024,128]{1,0:T(8,128)(2,1)S(1)} fusion(bf16[1024,1536]{1,0:T(8,128)(2,1)} %get-tuple-element.26, bf16[128,384]{1,0:T(8,128)(2,1)S(1)} %bitcast.92, bf16[128,384]{1,0:T(8,128)(2,1)S(1)} %bitcast.93, bf16[128,384]{1,0:T(8,128)(2,1)S(1)} %bitcast.94, bf16[128,384]{1,0:T(8,128)(2,1)S(1)} %bitcast.91), kind=kOutput, calls=%fused_computation.18 | convolution fusion | flops 404357120 | bytes 3801088 | tf_op jit(solution)/shard_map/dot_general | solution.py:15
  128.4 1.9 multiply_convert_fusion
  132.0 7.2 %convolution_convert_fusion = bf16[1024,1536]{1,0:T(8,128)(2,1)} fusion(bf16[1536,384]{1,0:T(8,128)(2,1)S(1)} %bitcast.78, s32[]{:T(128)S(6)} %select_n.7, bf16[1024,128]{0,1:T(8,128)(2,1)S(1)} %get-tuple-element.16, bf16[1024,128]{0,1:T(8,128)(2,1)S(1)} %get-tuple-element.15, bf16[1024,128]{0,1:T(8,128)(2,1)S(1)} %convolution_convert_fusion.4), kind=kOutput, calls=%fused_computation.3 | convolution fusion | flops 1214251008 | bytes 5111812 | tf_op jit(solution)/shard_map/dot_general | solution.py:15
  139.3 3.7 %convolution_convert_fusion.1 = bf16[1536,384]{1,0:T(8,128)(2,1)S(1)} fusion(bf16[1024,1536]{1,0:T(8,128)(2,1)} %copy-done.4, bf16[1024,128]{0,1:T(8,128)(2,1)S(1)} %convolution_convert_fusion.4, bf16[1024,128]{0,1:T(8,128)(2,1)S(1)} %get-tuple-element.15, bf16[1024,128]{0,1:T(8,128)(2,1)S(1)} %get-tuple-element.16), kind=kOutput, calls=%fused_computation.6 | convolution fusion | flops 1210908672 | bytes 5111808 | tf_op jit(solution)/shard_map/dot_general | solution.py:15
  143.1 5.3 %convolution_convert_fusion.2 = bf16[128,1536]{1,0:T(8,128)(2,1)S(1)} fusion(bf16[1024,1536]{1,0:T(8,128)(2,1)} %get-tuple-element.26, f32[1024,384]{0,1:T(8,128)S(1)} %fusion.49, f32[1024,1024]{0,1:T(8,128)} %copy-done.1, f32[1024]{0:T(1024)S(1)} %get-tuple-element.59, s32[1024]{0:T(1024)S(1)} %fusion.36), kind=kOutput, calls=%fused_computation.7 | convolution fusion | flops 676659200 | bytes 8007680 | tf_op jit(solution)/shard_map/dot_general | solution.py:15
  148.6 18.2 %all_to_all.10 = bf16[8,256,384]{2,1,0:T(8,128)(2,1)S(1)} all-to-all(bf16[8,256,384]{2,1,0:T(8,128)(2,1)S(1)} %constant_dynamic-update-slice_fusion.2), channel_id=1, replica_groups=mesh['dp'=8,'pipe'=4,'tensor'=16] {'dp'}, dimensions={0} | all-to-all | bytes 3145728 | tf_op jit(solution)/shard_map/all_to_all | solution.py:110
  167.2 17.7 %all_to_all.11 = bf16[8,256,384]{2,1,0:T(8,128)(2,1)S(1)} all-to-all(bf16[8,256,384]{2,1,0:T(8,128)(2,1)S(1)} %broadcast_in_dim.7), channel_id=1, replica_groups=mesh['dp'=8,'pipe'=4,'tensor'=16] {'dp'}, dimensions={0} | all-to-all | bytes 3145728 | tf_op jit(solution)/shard_map/all_to_all | solution.py:112
  186.1 24.7 %reduce-scatter.2.cloned.1.call-done = bf16[64,1536]{1,0:T(8,128)(2,1)} async-done(((bf16[1024,1536]{1,0:T(8,128)(2,1)}), bf16[64,1536]{1,0:T(8,128)(2,1)}) %reduce-scatter.2.cloned.1.call-update) | async-done | bytes 196624 | tf_op jit(solution)/shard_map/reduce_scatter | solution.py:105
  213.2 11.5 %collective-permute-start.15 = (bf16[64,1536]{1,0:T(8,128)(2,1)S(1)}, bf16[64,1536]{1,0:T(8,128)(2,1)S(1)}, u32[]{:S(2)}, u32[]{:S(2)}) collective-permute-start(bf16[64,1536]{1,0:T(8,128)(2,1)S(1)} %fusion.25), channel_id=1, source_target_pairs={{0,48},{16,0},{32,16},{48,32},{1,49},{17,1},{33,17},{49,33},{2,50}... | collective-permute-start | bytes 589832 | tf_op jit(solution)/shard_map/ppermute | solution.py:11
  225.5 5.3 %collective-permute-done.15 = bf16[64,1536]{1,0:T(8,128)(2,1)S(1)} collective-permute-done((bf16[64,1536]{1,0:T(8,128)(2,1)S(1)}, bf16[64,1536]{1,0:T(8,128)(2,1)S(1)}, u32[]{:S(2)}, u32[]{:S(2)}) %collective-permute-start.15) | collective-permute-done | bytes 196640 | tf_op jit(solution)/shard_map/ppermute | solution.py:11
  (82 shorter events, 38.1 us)
Async XLA Ops:
  7.2 86.0 %all-gather.3.cloned.1.call-start = ((), (), s32[]{:S(2)}) async-start(), calls=%async_computation.4 | async-start | bytes 1769472 | tf_op jit(solution)/shard_map/all_gather | solution.py:58
  12.1 19.7 %collective-permute-start = (bf16[128,1536]{1,0:T(8,128)(2,1)S(1)}, bf16[128,1536]{1,0:T(8,128)(2,1)S(1)}, u32[]{:S(2)}, u32[]{:S(2)}) collective-permute-start(bf16[128,1536]{1,0:T(8,128)(2,1)S(1)} %pad_maximum_fusion), channel_id=1, source_target_pairs={{0,15},{1,0},{2,1},{3,2},{4,3},{5,4},{6,5},{7,6},{8,7},{9,8},{10,9... | collective-permute-start | bytes 1179656 | tf_op jit(solution)/shard_map/ppermute | solution.py:11
  24.1 13.1 %collective-permute-start.7 = (bf16[128,1536]{1,0:T(8,128)(2,1)S(1)}, bf16[128,1536]{1,0:T(8,128)(2,1)S(1)}, u32[]{:S(2)}, u32[]{:S(2)}) collective-permute-start(bf16[128,1536]{1,0:T(8,128)(2,1)S(1)} %pad_maximum_fusion), channel_id=1, source_target_pairs={{0,1},{1,2},{2,3},{3,4},{4,5},{5,6},{6,7},{7,8},{8,9},{9,10},{10,1... | collective-permute-start | bytes 1179656 | tf_op jit(solution)/shard_map/ppermute | solution.py:11
  28.4 182.4 %reduce-scatter.2.cloned.1.call-start = ((), (), s32[]{:S(2)}) async-start(), calls=%async_computation.3 | async-start | bytes 3342336 | tf_op jit(solution)/shard_map/reduce_scatter | solution.py:105
  31.8 12.2 %collective-permute-start.1 = (bf16[128,1536]{1,0:T(8,128)(2,1)S(1)}, bf16[128,1536]{1,0:T(8,128)(2,1)S(1)}, u32[]{:S(2)}, u32[]{:S(2)}) collective-permute-start(bf16[128,1536]{1,0:T(8,128)(2,1)S(1)} %collective-permute-done), channel_id=1, source_target_pairs={{0,15},{1,0},{2,1},{3,2},{4,3},{5,4},{6,5},{7,6},{8,7},{9,8},{10,9... | collective-permute-start | bytes 1179656 | tf_op jit(solution)/shard_map/ppermute | solution.py:11
  37.2 12.1 %collective-permute-start.8 = (bf16[128,1536]{1,0:T(8,128)(2,1)S(1)}, bf16[128,1536]{1,0:T(8,128)(2,1)S(1)}, u32[]{:S(2)}, u32[]{:S(2)}) collective-permute-start(bf16[128,1536]{1,0:T(8,128)(2,1)S(1)} %collective-permute-done.7), channel_id=1, source_target_pairs={{0,1},{1,2},{2,3},{3,4},{4,5},{5,6},{6,7},{7,8},{8,9},{9,10},{10,1... | collective-permute-start | bytes 1179656 | tf_op jit(solution)/shard_map/ppermute | solution.py:11
  44.0 11.2 %collective-permute-start.2 = (bf16[128,1536]{1,0:T(8,128)(2,1)S(1)}, bf16[128,1536]{1,0:T(8,128)(2,1)S(1)}, u32[]{:S(2)}, u32[]{:S(2)}) collective-permute-start(bf16[128,1536]{1,0:T(8,128)(2,1)S(1)} %collective-permute-done.1), channel_id=1, source_target_pairs={{0,15},{1,0},{2,1},{3,2},{4,3},{5,4},{6,5},{7,6},{8,7},{9,8},{10,9... | collective-permute-start | bytes 1179656 | tf_op jit(solution)/shard_map/ppermute | solution.py:11
  49.3 11.2 %collective-permute-start.9 = (bf16[128,1536]{1,0:T(8,128)(2,1)S(1)}, bf16[128,1536]{1,0:T(8,128)(2,1)S(1)}, u32[]{:S(2)}, u32[]{:S(2)}) collective-permute-start(bf16[128,1536]{1,0:T(8,128)(2,1)S(1)} %collective-permute-done.8), channel_id=1, source_target_pairs={{0,1},{1,2},{2,3},{3,4},{4,5},{5,6},{6,7},{7,8},{8,9},{9,10},{10,1... | collective-permute-start | bytes 1179656 | tf_op jit(solution)/shard_map/ppermute | solution.py:11
  55.2 10.3 %collective-permute-start.3 = (bf16[128,1536]{1,0:T(8,128)(2,1)S(1)}, bf16[128,1536]{1,0:T(8,128)(2,1)S(1)}, u32[]{:S(2)}, u32[]{:S(2)}) collective-permute-start(bf16[128,1536]{1,0:T(8,128)(2,1)S(1)} %collective-permute-done.2), channel_id=1, source_target_pairs={{0,15},{1,0},{2,1},{3,2},{4,3},{5,4},{6,5},{7,6},{8,7},{9,8},{10,9... | collective-permute-start | bytes 1179656 | tf_op jit(solution)/shard_map/ppermute | solution.py:11
  60.6 10.4 %collective-permute-start.10 = (bf16[128,1536]{1,0:T(8,128)(2,1)S(1)}, bf16[128,1536]{1,0:T(8,128)(2,1)S(1)}, u32[]{:S(2)}, u32[]{:S(2)}) collective-permute-start(bf16[128,1536]{1,0:T(8,128)(2,1)S(1)} %collective-permute-done.9), channel_id=1, source_target_pairs={{0,1},{1,2},{2,3},{3,4},{4,5},{5,6},{6,7},{7,8},{8,9},{9,10},{10,1... | collective-permute-start | bytes 1179656 | tf_op jit(solution)/shard_map/ppermute | solution.py:11
  65.5 10.1 %collective-permute-start.4 = (bf16[128,1536]{1,0:T(8,128)(2,1)S(1)}, bf16[128,1536]{1,0:T(8,128)(2,1)S(1)}, u32[]{:S(2)}, u32[]{:S(2)}) collective-permute-start(bf16[128,1536]{1,0:T(8,128)(2,1)S(1)} %collective-permute-done.3), channel_id=1, source_target_pairs={{0,15},{1,0},{2,1},{3,2},{4,3},{5,4},{6,5},{7,6},{8,7},{9,8},{10,9... | collective-permute-start | bytes 1179656 | tf_op jit(solution)/shard_map/ppermute | solution.py:11
  71.0 9.7 %collective-permute-start.11 = (bf16[128,1536]{1,0:T(8,128)(2,1)S(1)}, bf16[128,1536]{1,0:T(8,128)(2,1)S(1)}, u32[]{:S(2)}, u32[]{:S(2)}) collective-permute-start(bf16[128,1536]{1,0:T(8,128)(2,1)S(1)} %collective-permute-done.10), channel_id=1, source_target_pairs={{0,1},{1,2},{2,3},{3,4},{4,5},{5,6},{6,7},{7,8},{8,9},{9,10},{10,1... | collective-permute-start | bytes 1179656 | tf_op jit(solution)/shard_map/ppermute | solution.py:11
  75.7 9.7 %collective-permute-start.5 = (bf16[128,1536]{1,0:T(8,128)(2,1)S(1)}, bf16[128,1536]{1,0:T(8,128)(2,1)S(1)}, u32[]{:S(2)}, u32[]{:S(2)}) collective-permute-start(bf16[128,1536]{1,0:T(8,128)(2,1)S(1)} %collective-permute-done.4), channel_id=1, source_target_pairs={{0,15},{1,0},{2,1},{3,2},{4,3},{5,4},{6,5},{7,6},{8,7},{9,8},{10,9... | collective-permute-start | bytes 1179656 | tf_op jit(solution)/shard_map/ppermute | solution.py:11
  80.7 9.7 %collective-permute-start.12 = (bf16[128,1536]{1,0:T(8,128)(2,1)S(1)}, bf16[128,1536]{1,0:T(8,128)(2,1)S(1)}, u32[]{:S(2)}, u32[]{:S(2)}) collective-permute-start(bf16[128,1536]{1,0:T(8,128)(2,1)S(1)} %collective-permute-done.11), channel_id=1, source_target_pairs={{0,1},{1,2},{2,3},{3,4},{4,5},{5,6},{6,7},{7,8},{8,9},{9,10},{10,1... | collective-permute-start | bytes 1179656 | tf_op jit(solution)/shard_map/ppermute | solution.py:11
  85.4 18.4 %collective-permute-start.6 = (bf16[128,1536]{1,0:T(8,128)(2,1)S(1)}, bf16[128,1536]{1,0:T(8,128)(2,1)S(1)}, u32[]{:S(2)}, u32[]{:S(2)}) collective-permute-start(bf16[128,1536]{1,0:T(8,128)(2,1)S(1)} %collective-permute-done.5), channel_id=1, source_target_pairs={{0,15},{1,0},{2,1},{3,2},{4,3},{5,4},{6,5},{7,6},{8,7},{9,8},{10,9... | collective-permute-start | bytes 1179656 | tf_op jit(solution)/shard_map/ppermute | solution.py:11
  90.4 10.3 %collective-permute-start.13 = (bf16[128,1536]{1,0:T(8,128)(2,1)S(1)}, bf16[128,1536]{1,0:T(8,128)(2,1)S(1)}, u32[]{:S(2)}, u32[]{:S(2)}) collective-permute-start(bf16[128,1536]{1,0:T(8,128)(2,1)S(1)} %collective-permute-done.12), channel_id=1, source_target_pairs={{0,1},{1,2},{2,3},{3,4},{4,5},{5,6},{6,7},{7,8},{8,9},{9,10},{10,1... | collective-permute-start | bytes 1179656 | tf_op jit(solution)/shard_map/ppermute | solution.py:11
  93.1 10.6 %copy-start.3 = (bf16[1024,1536]{1,0:T(8,128)(2,1)S(1)}, bf16[1024,1536]{1,0:T(8,128)(2,1)}, u32[]{:S(2)}) copy-start(bf16[1024,1536]{1,0:T(8,128)(2,1)} %get-tuple-element.43) | copy-start | bytes 9437188
  100.7 11.4 %collective-permute-start.14 = (bf16[128,1536]{1,0:T(8,128)(2,1)S(1)}, bf16[128,1536]{1,0:T(8,128)(2,1)S(1)}, u32[]{:S(2)}, u32[]{:S(2)}) collective-permute-start(bf16[128,1536]{1,0:T(8,128)(2,1)S(1)} %collective-permute-done.13), channel_id=1, source_target_pairs={{0,1},{1,2},{2,3},{3,4},{4,5},{5,6},{6,7},{7,8},{8,9},{9,10},{10,1... | collective-permute-start | bytes 1179656 | tf_op jit(solution)/shard_map/ppermute | solution.py:11
  117.8 1.8 copy-start.4
  117.8 1.9 copy-start.5
  117.8 1.9 copy-start.6
  120.8 7.5 %copy-start.1 = (f32[1024,1024]{0,1:T(8,128)}, f32[1024,1024]{0,1:T(8,128)S(1)}, u32[]{:S(2)}) copy-start(f32[1024,1024]{0,1:T(8,128)S(1)} %get-tuple-element.60) | copy-start | bytes 12582916
  167.2 43.6 %copy-start = (bf16[1,1,64,1536]{3,2,1,0:T(8,128)(2,1)S(1)}, bf16[1,1,64,1536]{3,2,1,0:T(8,128)(2,1)}, u32[]{:S(2)}) copy-start(bf16[1,1,64,1536]{3,2,1,0:T(8,128)(2,1)} %param.7) | copy-start | bytes 589828
  167.2 44.8 %copy-start.2 = (bf16[1,1,64,1536]{3,2,1,0:T(8,128)(2,1)S(1)}, bf16[1,1,64,1536]{3,2,1,0:T(8,128)(2,1)}, u32[]{:S(2)}) copy-start(bf16[1,1,64,1536]{3,2,1,0:T(8,128)(2,1)} %param.8) | copy-start | bytes 589828
  213.2 17.6 %collective-permute-start.15 = (bf16[64,1536]{1,0:T(8,128)(2,1)S(1)}, bf16[64,1536]{1,0:T(8,128)(2,1)S(1)}, u32[]{:S(2)}, u32[]{:S(2)}) collective-permute-start(bf16[64,1536]{1,0:T(8,128)(2,1)S(1)} %fusion.25), channel_id=1, source_target_pairs={{0,48},{16,0},{32,16},{48,32},{1,49},{17,1},{33,17},{49,33},{2,50}... | collective-permute-start | bytes 589832 | tf_op jit(solution)/shard_map/ppermute | solution.py:11
Sparse Core Ops, SparseCore 0:
  28.5 39.3 all-gather.2
  139.4 71.3 reduce-scatter.1

commit v2 on v1

v2 whole, which is shorter than its diff:
```python
import jax
import jax.numpy as jnp
from jax import lax
from jax.experimental import pallas as pl
from jax.experimental.pallas import tpu as pltpu
from jax.sharding import PartitionSpec as P

EPS = 1e-06
BLOCK = 256
TOP = 30000.0
LEAST = 1e-30


def shifted(array, axis, by):
    peers = lax.axis_size(axis)
    return lax.ppermute(array, axis, [(i, (i + by) % peers) for i in range(peers)])


def contract(left, right, left_dim, right_dim):
    return lax.dot_general(
        left, right, (((left_dim,), (right_dim,)), ((), ())), preferred_element_type=jnp.float32
    )


def fold_wide(wide, parts, width):
    rows, cols = wide.shape
    cut = [wide[:, c : c + width].reshape(parts, rows // parts, width) for c in range(0, cols, width)]
    return jnp.concatenate(cut, axis=1)


def unfold_wide(folded, cols):
    parts, rows, width = folded.shape
    high = rows * width // cols
    cut = [folded[:, i * high : (i + 1) * high].reshape(parts * high, width) for i in range(cols // width)]
    return jnp.concatenate(cut, axis=1)


def head_kernel(
    normed, cot, proj, outw, seg_col, seg_row, q_gain, k_gain,
    term, d_joined, attended,
    q_unit, k_unit, q_rate, k_rate, q_norm, k_norm, v_low, d_att, d_key, d_val,
):
    tokens, width = q_norm.shape
    factor = width ** (-0.5)
    count = tokens // BLOCK
    for i in range(count):
        rows = pl.ds(i * BLOCK, BLOCK)
        joined = jnp.dot(normed[rows, :], proj[...], preferred_element_type=jnp.float32)
        for at, unit, rate, norm, gain in (
            (0, q_unit, q_rate, q_norm, q_gain),
            (1, k_unit, k_rate, k_norm, k_gain),
        ):
            part = joined[:, at * width : (at + 1) * width]
            r = lax.rsqrt(jnp.mean(part * part, axis=-1, keepdims=True) + EPS)
            u = part * r
            rate[rows, :] = r
            unit[rows, :] = u
            norm[rows, :] = (u * gain[...]).astype(jnp.bfloat16)
        v_low[rows, :] = joined[:, 2 * width :].astype(jnp.bfloat16)
        d_att[rows, :] = contract(cot[rows, :], outw[...], 1, 1).astype(jnp.bfloat16)
    d_key[...] = jnp.zeros_like(d_key)
    d_val[...] = jnp.zeros_like(d_val)
    for i in range(count):
        rows = pl.ds(i * BLOCK, BLOCK)
        low, high = max(i - 1, 0), min(i + 2, count)
        near = pl.ds(low * BLOCK, (high - low) * BLOCK)
        qn, kn, vb, do = q_norm[rows, :], k_norm[near, :], v_low[near, :], d_att[rows, :]
        scores = contract(qn, kn, 1, 1) * factor
        same = seg_col[rows, :] == seg_row[:, low * BLOCK : high * BLOCK]
        expd = jnp.where(same, jnp.exp(scores), 0.0)
        probs = expd / jnp.sum(expd, axis=-1, keepdims=True)
        probs_low = probs.astype(jnp.bfloat16)
        attended[rows, :] = jnp.dot(probs_low, vb, preferred_element_type=jnp.float32).astype(jnp.bfloat16)
        d_probs = contract(do, vb, 1, 1)
        d_val[near, :] += contract(probs_low, do, 0, 0)
        delta = jnp.sum(probs * d_probs, axis=-1, keepdims=True)
        d_scores = (probs * (d_probs - delta) * factor).astype(jnp.bfloat16)
        d_key[near, :] += contract(d_scores, qn, 0, 0)
        back = jnp.dot(d_scores, kn, preferred_element_type=jnp.float32) * q_gain[...]
        u = q_unit[rows, :]
        d_query = q_rate[rows, :] * (back - u * jnp.mean(back * u, axis=-1, keepdims=True))
        d_joined[rows, 0:width] = d_query.astype(jnp.bfloat16)
    for i in range(count):
        rows = pl.ds(i * BLOCK, BLOCK)
        back = d_key[rows, :] * k_gain[...]
        u = k_unit[rows, :]
        d_keys = k_rate[rows, :] * (back - u * jnp.mean(back * u, axis=-1, keepdims=True))
        d_joined[rows, width : 2 * width] = d_keys.astype(jnp.bfloat16)
        d_joined[rows, 2 * width :] = d_val[rows, :].astype(jnp.bfloat16)
        term[rows, :] = contract(d_joined[rows, :], proj[...], 1, 1).astype(jnp.bfloat16)


def head_backward(normed, cotangent, proj, outw, segments, q_scale, k_scale):
    tokens, features = normed.shape
    width = outw.shape[0]
    here = pl.BlockSpec(memory_space=pltpu.VMEM)

    def kept(columns, dtype):
        return pltpu.VMEM((tokens, columns), dtype)

    return pl.pallas_call(
        head_kernel,
        out_shape=(
            jax.ShapeDtypeStruct((tokens, features), jnp.bfloat16),
            jax.ShapeDtypeStruct((tokens, 3 * width), jnp.bfloat16),
            jax.ShapeDtypeStruct((tokens, width), jnp.bfloat16),
        ),
        in_specs=[here] * 8,
        out_specs=(here,) * 3,
        scratch_shapes=[
            kept(width, jnp.float32), kept(width, jnp.float32), kept(1, jnp.float32), kept(1, jnp.float32),
            kept(width, jnp.bfloat16), kept(width, jnp.bfloat16), kept(width, jnp.bfloat16), kept(width, jnp.bfloat16),
            kept(width, jnp.float32), kept(width, jnp.float32),
        ],
        compiler_params=pltpu.CompilerParams(vmem_limit_bytes=40 * 1024 * 1024),
        cost_estimate=pl.CostEstimate(flops=5_000_000_000, bytes_accessed=12_000_000, transcendentals=1_000_000),
    )(
        normed, cotangent, proj, outw, segments[:, None], segments[None, :], q_scale[None, :], k_scale[None, :]
    )


def per_device(saved_input, grad_in, segment_ids, w_qkv, w_out, q_gain, k_gain):
    dp = lax.axis_size("dp")
    me = lax.axis_index("tensor")
    x_float = saved_input[0, 0].astype(jnp.float32)
    rows = x_float.shape[0]
    centred = x_float - jnp.mean(x_float, axis=-1, keepdims=True)
    scaled = lax.rsqrt(jnp.mean(centred * centred, axis=-1, keepdims=True) + EPS)
    unit = centred * scaled
    cot_rows = grad_in[0, 0]
    three = w_qkv.shape[3]
    share = w_qkv.shape[1]
    weights = jnp.concatenate([w_qkv[0, :, 0, :], fold_wide(w_out[0, 0], 1, three)[0]], axis=0)
    weights = lax.all_gather(weights, "dp", axis=0)
    proj_full = weights[:, :share].reshape(dp * share, three)
    outw_full = unfold_wide(weights[:, share:], w_out.shape[3])
    low_rows = unit.astype(jnp.bfloat16)
    scales = [TOP / jnp.maximum(jnp.max(jnp.abs(b.astype(jnp.float32))), LEAST) for b in (low_rows, cot_rows)]
    sent = [(b.astype(jnp.float32) * s).astype(jnp.float16) for b, s in zip((low_rows, cot_rows), scales)]
    blocks = lax.all_gather(jnp.concatenate(sent, axis=0), "tensor", axis=0)
    peers = blocks.shape[0]
    table = jnp.zeros((peers * 16, 128), jnp.float32)
    mine = jnp.where(lax.broadcasted_iota(jnp.int32, (16, 128), 1) < 64, scales[0], scales[1])
    table = lax.psum(lax.dynamic_update_slice(table, mine, (me * 16, 0)), "tensor")
    inverse = 1.0 / table.reshape(peers, 16, 128)[:, :1, :]
    normed = (blocks[:, :rows].astype(jnp.float32) * inverse[:, :, :1]).astype(jnp.bfloat16)
    cotangent = (blocks[:, rows:].astype(jnp.float32) * inverse[:, :, 64:65]).astype(jnp.bfloat16)
    normed = normed.reshape(peers * rows, normed.shape[-1])
    cotangent = cotangent.reshape(peers * rows, cotangent.shape[-1])
    term, d_joined, attended = head_backward(
        normed, cotangent, proj_full, outw_full, segment_ids[0, 0], q_gain[0], k_gain[0]
    )
    d_outw = contract(attended, cotangent, 0, 0)
    d_normed = lax.psum_scatter(term, "tensor", scatter_dimension=0, tiled=True).astype(jnp.float32)
    d_proj = contract(normed, d_joined, 0, 0).astype(jnp.bfloat16)
    gradients = jnp.concatenate(
        [d_proj.reshape(dp, share, three), fold_wide(d_outw.astype(jnp.bfloat16), dp, three)], axis=1
    )
    terms = lax.all_to_all(gradients, "dp", 0, 0)
    total = jnp.sum(terms.astype(jnp.float32), axis=0).astype(jnp.bfloat16)
    sums = lax.all_to_all(jnp.broadcast_to(total[None], terms.shape), "dp", 0, 0)
    grad_qkv = sums[:, :share].reshape(dp * share, three)
    grad_wout = unfold_wide(sums[:, share:], w_out.shape[3])
    d_tokens = cot_rows.astype(jnp.float32) + scaled * (
        d_normed
        - jnp.mean(d_normed, axis=-1, keepdims=True)
        - unit * jnp.mean(d_normed * unit, axis=-1, keepdims=True)
    )
    passed = shifted(d_tokens.astype(jnp.bfloat16), "pipe", -1)
    return passed[None, None], grad_qkv[None, :, None, :], grad_wout[None, None]


def solution(mesh):
    placed = (
        P("dp", "pipe", "tensor", None),
        P("dp", "pipe", "tensor", None),
        P("dp", "pipe", None),
        P("pipe", "dp", "tensor", None),
        P("pipe", "tensor", "dp", None),
        P("pipe", None),
        P("pipe", None),
    )
    return jax.shard_map(
        per_device,
        mesh=mesh,
        in_specs=placed,
        out_specs=(
            P("dp", "pipe", "tensor", None),
            P("pipe", None, "tensor", None),
            P("pipe", "tensor", None, None),
        ),
        check_vma=False,
    )
```

time: 239 us -> 270 us (1.13)
  blocking collectives: 35.9 us -> 118 us
  starting transfers between devices: 70.3 us -> 11.9 us
  waiting for transfers between devices: 58.1 us -> 82.1 us
  matrix products: 27.8 us -> 4.51 us
  Pallas kernels: 0 us -> 8.45 us
  local copies, waits for them, and re-layouts: 18.8 us -> 10.9 us
  other arithmetic: 13 us -> 16.5 us
    all_gather x0 -> x1, blocking collectives: none -> 81.8 us  [per_device(): blocks = lax.all_gather(jnp.concatenate(sent, axis=0), 'tensor', axis=0)]
    ppermute x16 -> x1, starting transfers between devices: 70.2 us -> 11.8 us  [shifted(): lax.ppermute(array, axis, [(i, (i + by) % peers) for i in range(peers)])]
    psum x0 -> x1, waiting for transfers between devices: none -> 46.1 us  [per_device(): lax.psum(lax.dynamic_update_slice(table, mine, (me * 16, 0)), 'tensor')]
    ppermute x16 -> x1, waiting for transfers between devices: 33.4 us -> 5.03 us  [shifted(): lax.ppermute(array, axis, [(i, (i + by) % peers) for i in range(peers)])]
    dot_general x8 -> x2, matrix products: 25.9 us -> 4.51 us  [contract(): lax.dot_general(left, right, (((left_dim,), (right_dim,)), ((), ())), pre...]
    unnamed x34 -> x29, local copies, waits for them, and re-layouts: 13.3 us -> 4.72 us
    pallas_call x0 -> x1, Pallas kernels: none -> 8.45 us  [head_backward(): pl.pallas_call(head_kernel, out_shape=(jax.ShapeDtypeStruct((tokens, feat...]
    reduce_scatter x1, waiting for transfers between devices: 24.7 us -> 30.9 us  [per_device(): lax.psum_scatter(term, 'tensor', scatter_dimension=0, tiled=True)]
  transfers between devices with their start and end apart: 18 -> 4, of which waited for: 10 -> 3; matrix products, arithmetic and copies ran while one was open for 10% -> 6% of each run, Pallas kernels for 0% -> 0%
where the time goes in v2:
time: 270 us
  blocking collectives  118 us (44%)
  waiting for transfers between devices  82.1 us (30%)
  between operations  17.2 us (6%)
  other arithmetic  16.5 us (6%)
  starting transfers between devices  11.9 us (4%)
  local copies, waits for them, and re-layouts  10.9 us (4%)
  Pallas kernels  8.45 us (3%)
  matrix products  4.51 us (2%)
    all_gather x1, blocking collectives, per_device(): blocks = lax.all_gather(jnp.concatenate(sent, axis=0), 'tensor', axis=0)  81.8 us
    psum x1, waiting for transfers between devices, per_device(): lax.psum(lax.dynamic_update_slice(table, mine, (me * 16, 0)), 'tensor')  46.1 us
    reduce_scatter x1, waiting for transfers between devices, per_device(): lax.psum_scatter(term, 'tensor', scatter_dimension=0, tiled=True)  30.9 us
    all_to_all x1, blocking collectives, per_device(): lax.all_to_all(jnp.broadcast_to(total[None], terms.shape), 'dp', 0, 0)  18.5 us
    all_to_all x1, blocking collectives, per_device(): terms = lax.all_to_all(gradients, 'dp', 0, 0)  17.9 us
    ppermute x1, starting transfers between devices, shifted(): lax.ppermute(array, axis, [(i, (i + by) % peers) for i in range(peers)])  11.8 us
    pallas_call x1, Pallas kernels, head_backward(): pl.pallas_call(head_kernel, out_shape=(jax.ShapeDtypeStruct((tokens, feat...  8.45 us
  transfers between devices with their start and end apart: 4, of which 3 were waited for; matrix products, arithmetic and copies ran while one was open for 6% of the time, Pallas kernels for 0%

profile of v2, /device:TPU:1, one launch (start us, length us, event | category | flops | bytes accessed | tf_op | source)
XLA Modules:
  0.0 269.6 jit_solution(14278640024749368744)
XLA Ops:
  8.1 1.2 convert_reduce_fusion.1
  9.3 1.2 fusion.7
  10.4 1.7 fusion.8
  12.1 1.6 fusion.11
  15.1 0.6 copy-done.11
  15.8 0.8 slice_bitcast_fusion.3
  16.6 1.6 pad_maximum_fusion.2
  18.5 1.0 copy.11.seg_col
  19.6 81.8 %all-gather.6 = f16[2048,1536]{1,0:T(8,128)(2,1)} all-gather(f16[128,1536]{1,0:T(8,128)(2,1)S(1)} %pad_maximum_fusion), channel_id=2, replica_groups=mesh['dp'=8,'pipe'=4,'tensor'=16] {'tensor'}, dimensions={0}, use_global_device_ids=true | all-gather | bytes 6684672 | tf_op jit(solution)/shard_map/all_gather | solution.py:140
  101.5 46.1 %all-reduce.2.cloned.1.call-done = f32[16,16,128]{2,1,0:T(8,128)} async-done(((f32[16,16,128]{2,1,0:T(8,128)}), f32[16,16,128]{2,1,0:T(8,128)}) %all-reduce.2.cloned.1.call-update) | async-done | bytes 131088 | tf_op jit(solution)/shard_map/psum | solution.py:144
  147.6 0.9 slice_divide_fusion
  148.5 0.3 slice_reduce_fusion
  148.8 4.7 %multiply_convert_fusion = (bf16[16,64,1536]{2,1,0:T(8,128)(2,1)S(1)}, bf16[16,64,1536]{2,1,0:T(8,128)(2,1)}) fusion(f16[16,128,1536]{2,1,0:T(8,128)(2,1)} %bitcast.83, f32[16]{0:T(128)S(1)} %get-tuple-element.11, f32[16]{0:T(128)S(1)} %get-tuple-element.12), kind=kLoop, calls=%fused_computation | loop fusion | flops 9437184 | bytes 12583040 | tf_op jit(solution)/shard_map/convert_element_type | solution.py:147
  153.5 1.1 fusion.15
  154.7 1.5 slice.111
  156.3 0.6 copy-done.1
  156.9 8.5 %shard_map.94 = (bf16[1024,1536]{1,0:T(8,128)(2,1)S(1)}, bf16[1024,384]{1,0:T(8,128)(2,1)S(1)}, bf16[1024,128]{1,0:T(8,128)(2,1)S(1)}) custom-call(bf16[1024,1536]{1,0:T(8,128)(2,1)S(1)} %bitcast.79, bf16[1024,1536]{1,0:T(8,128)(2,1)S(1)} %bitcast.76, bf16[1536,384]{1,0:T(8,128)(2,1)S(1)} %bitcast.80, bf16[128,1536]{1,0:T(8,128)(2,1)S(1)} %pad_maximum_fusion.1.outw, ...), custom_call_target="tpu_custom_call" | custom-call | flops 5000000000 | bytes 12000000 | tf_op jit(solution)/shard_map/pallas_call | solution.py:101
  165.4 1.7 copy-done
  167.0 0.9 copy-done.6
  167.9 3.9 %convolution_convert_fusion = bf16[1536,384]{1,0:T(8,128)(2,1)S(1)} fusion(bf16[1024,1536]{1,0:T(8,128)(2,1)} %bitcast.78, bf16[1024,384]{1,0:T(8,128)(2,1)} %copy-done.6), kind=kOutput, calls=%fused_computation.2 | convolution fusion | flops 1208549376 | bytes 5111808 | tf_op jit(solution)/shard_map/dot_general | solution.py:20
  172.0 0.6 convolution_convert_fusion.1
  172.8 17.9 %all_to_all.10 = bf16[8,256,384]{2,1,0:T(8,128)(2,1)S(1)} all-to-all(bf16[8,256,384]{2,1,0:T(8,128)(2,1)S(1)} %constant_dynamic-update-slice_fusion), channel_id=1, replica_groups=mesh['dp'=8,'pipe'=4,'tensor'=16] {'dp'}, dimensions={0} | all-to-all | bytes 3145728 | tf_op jit(solution)/shard_map/all_to_all | solution.py:159
  190.6 0.3 reduce_sum.52
  191.0 18.5 %all_to_all.11 = bf16[8,256,384]{2,1,0:T(8,128)(2,1)S(1)} all-to-all(bf16[8,256,384]{2,1,0:T(8,128)(2,1)S(1)} %broadcast_in_dim.31), channel_id=1, replica_groups=mesh['dp'=8,'pipe'=4,'tensor'=16] {'dp'}, dimensions={0} | all-to-all | bytes 3145728 | tf_op jit(solution)/shard_map/all_to_all | solution.py:161
  209.5 1.1 slice.120
  210.7 30.9 %reduce-scatter.2.cloned.1.call-done = bf16[64,1536]{1,0:T(8,128)(2,1)} async-done(((bf16[1024,1536]{1,0:T(8,128)(2,1)}), bf16[64,1536]{1,0:T(8,128)(2,1)}) %reduce-scatter.2.cloned.1.call-update) | async-done | bytes 196624 | tf_op jit(solution)/shard_map/reduce_scatter | solution.py:154
  241.5 1.2 convert_reduce_fusion
  242.8 1.1 fusion.13
  243.9 11.8 %collective-permute-start = (bf16[64,1536]{1,0:T(8,128)(2,1)S(1)}, bf16[64,1536]{1,0:T(8,128)(2,1)S(1)}, u32[]{:S(2)}, u32[]{:S(2)}) collective-permute-start(bf16[64,1536]{1,0:T(8,128)(2,1)S(1)} %fusion.13), channel_id=1, source_target_pairs={{0,48},{16,0},{32,16},{48,32},{1,49},{17,1},{33,17},{49,33},{2,50}... | collective-permute-start | bytes 589832 | tf_op jit(solution)/shard_map/ppermute | solution.py:16
  255.7 0.8 maximum_bitcast_fusion
  256.5 5.0 %collective-permute-done = bf16[64,1536]{1,0:T(8,128)(2,1)S(1)} collective-permute-done((bf16[64,1536]{1,0:T(8,128)(2,1)S(1)}, bf16[64,1536]{1,0:T(8,128)(2,1)S(1)}, u32[]{:S(2)}, u32[]{:S(2)}) %collective-permute-start) | collective-permute-done | bytes 196640 | tf_op jit(solution)/shard_map/ppermute | solution.py:16
  261.5 0.7 copy.19
  (46 shorter events, 1.0 us)
Async XLA Ops:
  8.0 10.3 %copy-start.7 = (bf16[1,1,64,1536]{3,2,1,0:T(8,128)(2,1)S(1)}, bf16[1,1,64,1536]{3,2,1,0:T(8,128)(2,1)}, u32[]{:S(2)}) copy-start(bf16[1,1,64,1536]{3,2,1,0:T(8,128)(2,1)} %param.7) | copy-start | bytes 589828
  8.0 10.3 %copy-start.9 = (bf16[1,1,64,1536]{3,2,1,0:T(8,128)(2,1)S(1)}, bf16[1,1,64,1536]{3,2,1,0:T(8,128)(2,1)}, u32[]{:S(2)}) copy-start(bf16[1,1,64,1536]{3,2,1,0:T(8,128)(2,1)} %param.8) | copy-start | bytes 589828
  8.0 10.5 %copy-start.3 = (s32[1,1,1024]{2,1,0:T(1,128)S(1)}, s32[1,1,1024]{2,1,0:T(1,128)}, u32[]{:S(2)}) copy-start(s32[1,1,1024]{2,1,0:T(1,128)} %param.9) | copy-start | bytes 12292
  8.0 139.6 %all-reduce.2.cloned.1.call-start = ((), (), s32[]{:S(2)}) async-start(), calls=%async_computation.3 | async-start | bytes 262144 | tf_op jit(solution)/shard_map/psum | solution.py:144
  15.1 0.7 copy-start.11
  15.8 137.7 %all-gather.5.cloned.1.call-start = ((), (), s32[]{:S(2)}) async-start(), calls=%async_computation.5 | async-start | bytes 1769472 | tf_op jit(solution)/shard_map/all_gather | solution.py:134
  18.2 223.3 %reduce-scatter.2.cloned.1.call-start = ((), (), s32[]{:S(2)}) async-start(), calls=%async_computation.4 | async-start | bytes 3342336 | tf_op jit(solution)/shard_map/reduce_scatter | solution.py:154
  153.5 2.8 %copy-start.2 = (s32[1024,1]{1,0:T(8,128)S(1)}, s32[1024,1]{1,0:T(8,128)}, u32[]{:S(2)}) copy-start(s32[1024,1]{1,0:T(8,128)} %copy.11.seg_col) | copy-start | bytes 12292
  154.6 2.3 copy-start.1
  154.6 2.3 copy-start.4
  154.7 2.2 copy-start.5
  165.4 1.7 copy-start
  167.0 0.9 copy-start.6
  209.5 32.1 %copy-start.8 = (bf16[1,1,64,1536]{3,2,1,0:T(8,128)(2,1)S(1)}, bf16[1,1,64,1536]{3,2,1,0:T(8,128)(2,1)}, u32[]{:S(2)}) copy-start(bf16[1,1,64,1536]{3,2,1,0:T(8,128)(2,1)} %param.7) | copy-start | bytes 589828
  209.5 33.3 %copy-start.10 = (bf16[1,1,64,1536]{3,2,1,0:T(8,128)(2,1)S(1)}, bf16[1,1,64,1536]{3,2,1,0:T(8,128)(2,1)}, u32[]{:S(2)}) copy-start(bf16[1,1,64,1536]{3,2,1,0:T(8,128)(2,1)} %param.8) | copy-start | bytes 589828
  243.9 17.6 %collective-permute-start = (bf16[64,1536]{1,0:T(8,128)(2,1)S(1)}, bf16[64,1536]{1,0:T(8,128)(2,1)S(1)}, u32[]{:S(2)}, u32[]{:S(2)}) collective-permute-start(bf16[64,1536]{1,0:T(8,128)(2,1)S(1)} %fusion.13), channel_id=1, source_target_pairs={{0,48},{16,0},{32,16},{48,32},{1,49},{17,1},{33,17},{49,33},{2,50}... | collective-permute-start | bytes 589832 | tf_op jit(solution)/shard_map/ppermute | solution.py:16
Sparse Core Ops, SparseCore 0:
  15.9 131.6 all-reduce.1
  168.1 73.4 reduce-scatter.1
Sparse Core Ops, SparseCore 1:
  19.1 48.1 all-gather.4

commit v3 on v2

v3 whole, which is shorter than its diff:
```python
import functools

import jax
import jax.numpy as jnp
from jax import lax
from jax.experimental import pallas as pl
from jax.experimental.pallas import tpu as pltpu
from jax.sharding import PartitionSpec as P

EPS = 1e-06
BLOCK = 256


def shifted(array, axis, by):
    peers = lax.axis_size(axis)
    return lax.ppermute(array, axis, [(i, (i + by) % peers) for i in range(peers)])


def contract(left, right, left_dim, right_dim):
    return lax.dot_general(
        left, right, (((left_dim,), (right_dim,)), ((), ())), preferred_element_type=jnp.float32
    )


def ring_gather(block, axis):
    peers = lax.axis_size(axis)
    got = {0: block}
    up = down = block
    for step in range(1, peers // 2 + 1):
        up = shifted(up, axis, 1)
        got[peers - step] = up
        if step < peers - step:
            down = shifted(down, axis, -1)
            got[step] = down
    return [got[i] for i in range(peers)]


def fold_wide(wide, parts, width):
    rows, cols = wide.shape
    cut = [wide[:, c : c + width].reshape(parts, rows // parts, width) for c in range(0, cols, width)]
    return jnp.concatenate(cut, axis=1)


def unfold_wide(folded, cols):
    parts, rows, width = folded.shape
    high = rows * width // cols
    cut = [folded[:, i * high : (i + 1) * high].reshape(parts * high, width) for i in range(cols // width)]
    return jnp.concatenate(cut, axis=1)


def normalised(rows):
    x = rows.astype(jnp.float32)
    centred = x - jnp.mean(x, axis=-1, keepdims=True)
    rate = lax.rsqrt(jnp.mean(centred * centred, axis=-1, keepdims=True) + EPS)
    return centred * rate, rate


def first_kernel(tokens, cot, block):
    rows = tokens.shape[0]
    block[0:rows, :] = normalised(tokens[...])[0].astype(jnp.bfloat16)
    block[rows:, :] = cot[...]


def last_kernel(tokens, cot, d_normed, out):
    unit, rate = normalised(tokens[...])
    d = d_normed[...].astype(jnp.float32)
    inner = d - jnp.mean(d, axis=-1, keepdims=True) - unit * jnp.mean(d * unit, axis=-1, keepdims=True)
    out[...] = (cot[...].astype(jnp.float32) + rate * inner).astype(jnp.bfloat16)


def head_kernel(peers, where, weights, seg_col, seg_row, q_gain, k_gain, *rest):
    blocks, rest = rest[:peers], rest[peers:]
    term, d_joined, attended, normed, cot = rest[:5]
    (proj, outw, made, sems,
     q_unit, k_unit, q_rate, k_rate, q_norm, k_norm, v_low, d_att, d_key, d_val) = rest[5:]
    tokens, width = q_norm.shape
    share = proj.shape[0] // weights.shape[0]
    three = proj.shape[1]
    piece = width // weights.shape[0]
    for p in range(weights.shape[0]):
        proj[p * share : (p + 1) * share, :] = weights[p, 0:share, :]
        for c in range(outw.shape[1] // three):
            low = share + c * piece
            outw[p * piece : (p + 1) * piece, c * three : (c + 1) * three] = weights[p, low : low + piece, :]
    each = tokens // peers
    for d in range(peers):
        at = lax.rem(where[0, 0] + d, peers) * each
        at = pl.multiple_of(at, each)
        normed[pl.ds(at, each), :] = blocks[d][0:each, :]
        cot[pl.ds(at, each), :] = blocks[d][each:, :]
    factor = width ** (-0.5)
    count = tokens // BLOCK
    for i in range(count):
        rows = pl.ds(i * BLOCK, BLOCK)
        joined = jnp.dot(normed[rows, :], proj[...], preferred_element_type=jnp.float32)
        for at, unit, rate, norm, gain in (
            (0, q_unit, q_rate, q_norm, q_gain),
            (1, k_unit, k_rate, k_norm, k_gain),
        ):
            part = joined[:, at * width : (at + 1) * width]
            r = lax.rsqrt(jnp.mean(part * part, axis=-1, keepdims=True) + EPS)
            u = part * r
            rate[rows, :] = r
            unit[rows, :] = u
            norm[rows, :] = (u * gain[...]).astype(jnp.bfloat16)
        v_low[rows, :] = joined[:, 2 * width :].astype(jnp.bfloat16)
        d_att[rows, :] = contract(cot[rows, :], outw[...], 1, 1).astype(jnp.bfloat16)
    d_key[...] = jnp.zeros_like(d_key)
    d_val[...] = jnp.zeros_like(d_val)
    copies = []
    for i in range(count + 1):
        if i < count:
            rows = pl.ds(i * BLOCK, BLOCK)
            low, high = max(i - 1, 0), min(i + 2, count)
            near = pl.ds(low * BLOCK, (high - low) * BLOCK)
            qn, kn, vb, do = q_norm[rows, :], k_norm[near, :], v_low[near, :], d_att[rows, :]
            scores = contract(qn, kn, 1, 1) * factor
            same = seg_col[rows, :] == seg_row[:, low * BLOCK : high * BLOCK]
            expd = jnp.where(same, jnp.exp(scores), 0.0)
            probs = expd / jnp.sum(expd, axis=-1, keepdims=True)
            probs_low = probs.astype(jnp.bfloat16)
            attended[rows, :] = jnp.dot(probs_low, vb, preferred_element_type=jnp.float32).astype(jnp.bfloat16)
            d_probs = contract(do, vb, 1, 1)
            d_val[near, :] += contract(probs_low, do, 0, 0)
            delta = jnp.sum(probs * d_probs, axis=-1, keepdims=True)
            d_scores = (probs * (d_probs - delta) * factor).astype(jnp.bfloat16)
            d_key[near, :] += contract(d_scores, qn, 0, 0)
            back = jnp.dot(d_scores, kn, preferred_element_type=jnp.float32) * q_gain[...]
            u = q_unit[rows, :]
            d_query = q_rate[rows, :] * (back - u * jnp.mean(back * u, axis=-1, keepdims=True))
            d_joined[rows, 0:width] = d_query.astype(jnp.bfloat16)
        if i > 0:
            rows = pl.ds((i - 1) * BLOCK, BLOCK)
            back = d_key[rows, :] * k_gain[...]
            u = k_unit[rows, :]
            d_keys = k_rate[rows, :] * (back - u * jnp.mean(back * u, axis=-1, keepdims=True))
            d_joined[rows, width : 2 * width] = d_keys.astype(jnp.bfloat16)
            d_joined[rows, 2 * width :] = d_val[rows, :].astype(jnp.bfloat16)
            made[rows, :] = contract(d_joined[rows, :], proj[...], 1, 1).astype(jnp.bfloat16)
            copy = pltpu.make_async_copy(made.at[rows, :], term.at[rows, :], sems.at[i - 1])
            copy.start()
            copies.append(copy)
    for copy in copies:
        copy.wait()


def head_backward(blocks, weights, share, segments, q_scale, k_scale, me):
    peers = len(blocks)
    tokens = segments.shape[0]
    features = blocks[0].shape[1]
    width = q_scale.shape[0]
    here = pl.BlockSpec(memory_space=pltpu.VMEM)
    low = jnp.bfloat16

    def kept(columns, dtype):
        return pltpu.VMEM((tokens, columns), dtype)

    return pl.pallas_call(
        functools.partial(head_kernel, peers),
        out_shape=tuple(
            jax.ShapeDtypeStruct((tokens, columns), low) for columns in (features, 3 * width, width, features, features)
        ),
        in_specs=[pl.BlockSpec(memory_space=pltpu.SMEM)] + [here] * (5 + peers),
        out_specs=(pl.BlockSpec(memory_space=pl.ANY),) + (here,) * 4,
        scratch_shapes=[
            pltpu.VMEM((features, 3 * width), low), pltpu.VMEM((width, features), low), kept(features, low),
            pltpu.SemaphoreType.DMA((tokens // BLOCK,)),
            kept(width, jnp.float32), kept(width, jnp.float32), kept(1, jnp.float32), kept(1, jnp.float32),
            kept(width, low), kept(width, low), kept(width, low), kept(width, low),
            kept(width, jnp.float32), kept(width, jnp.float32),
        ],
        compiler_params=pltpu.CompilerParams(vmem_limit_bytes=48 * 1024 * 1024),
        cost_estimate=pl.CostEstimate(flops=5_000_000_000, bytes_accessed=12_000_000, transcendentals=1_000_000),
    )(
        me.reshape(1, 1), weights, segments[:, None], segments[None, :], q_scale[None, :], k_scale[None, :], *blocks
    )


def per_device(saved_input, grad_in, segment_ids, w_qkv, w_out, q_gain, k_gain):
    dp = lax.axis_size("dp")
    me = lax.axis_index("tensor").astype(jnp.int32)
    tokens, cot = saved_input[0, 0], grad_in[0, 0]
    three = w_qkv.shape[3]
    share = w_qkv.shape[1]
    here = pl.BlockSpec(memory_space=pltpu.VMEM)
    weights = jnp.concatenate([w_qkv[0, :, 0, :], fold_wide(w_out[0, 0], 1, three)[0]], axis=0)
    weights = lax.all_gather(weights, "dp", axis=0)
    block = pl.pallas_call(
        first_kernel,
        out_shape=jax.ShapeDtypeStruct((2 * tokens.shape[0], tokens.shape[1]), jnp.bfloat16),
        in_specs=[here, here],
        out_specs=here,
    )(tokens, cot)
    blocks = ring_gather(block, "tensor")
    term, d_joined, attended, normed, cotangent = head_backward(
        blocks, weights, share, segment_ids[0, 0], q_gain[0], k_gain[0], me
    )
    d_normed = lax.psum_scatter(term, "tensor", scatter_dimension=0, tiled=True)
    d_outw = contract(attended, cotangent, 0, 0)
    d_proj = contract(normed, d_joined, 0, 0).astype(jnp.bfloat16)
    gradients = jnp.concatenate(
        [d_proj.reshape(dp, share, three), fold_wide(d_outw.astype(jnp.bfloat16), dp, three)], axis=1
    )
    terms = lax.all_to_all(gradients, "dp", 0, 0)
    total = jnp.sum(terms.astype(jnp.float32), axis=0).astype(jnp.bfloat16)
    sums = lax.all_to_all(jnp.broadcast_to(total[None], terms.shape), "dp", 0, 0)
    grad_qkv = sums[:, :share].reshape(dp * share, three)
    grad_wout = unfold_wide(sums[:, share:], w_out.shape[3])
    d_tokens = pl.pallas_call(
        last_kernel,
        out_shape=jax.ShapeDtypeStruct(tokens.shape, jnp.bfloat16),
        in_specs=[here] * 3,
        out_specs=here,
    )(tokens, cot, d_normed)
    passed = shifted(d_tokens, "pipe", -1)
    return passed[None, None], grad_qkv[None, :, None, :], grad_wout[None, None]


def solution(mesh):
    placed = (
        P("dp", "pipe", "tensor", None),
        P("dp", "pipe", "tensor", None),
        P("dp", "pipe", None),
        P("pipe", "dp", "tensor", None),
        P("pipe", "tensor", "dp", None),
        P("pipe", None),
        P("pipe", None),
    )
    return jax.shard_map(
        per_device,
        mesh=mesh,
        in_specs=placed,
        out_specs=(
            P("dp", "pipe", "tensor", None),
            P("pipe", None, "tensor", None),
            P("pipe", "tensor", None, None),
        ),
        check_vma=False,
    )
```

time: 270 us -> 224 us (0.83)
  blocking collectives: 118 us -> 35.1 us
  starting transfers between devices: 11.9 us -> 69.5 us
  other arithmetic: 16.5 us -> 2.65 us
  waiting for transfers between devices: 82.1 us -> 68.8 us
  Pallas kernels: 8.45 us -> 19 us
  between operations: 17.2 us -> 14.4 us
    all_gather x1 -> x0, blocking collectives: 81.8 us -> none  [per_device(): blocks = lax.all_gather(jnp.concatenate(sent, axis=0), 'tensor', axis=0)]
    ppermute x1 -> x16, starting transfers between devices: 11.8 us -> 69.4 us  [shifted(): lax.ppermute(array, axis, [(i, (i + by) % peers) for i in range(peers)])]
    psum x1 -> x0, waiting for transfers between devices: 46.1 us -> none  [per_device(): lax.psum(lax.dynamic_update_slice(table, mine, (me * 16, 0)), 'tensor')]
    ppermute x1 -> x16, waiting for transfers between devices: 5.03 us -> 38.5 us  [shifted(): lax.ppermute(array, axis, [(i, (i + by) % peers) for i in range(peers)])]
    pallas_call x1 -> x3, Pallas kernels: 8.45 us -> 19 us  [the longest x1 14.8 us: head_backward(): pl.pallas_call(functools.partial(head_kernel, peers), out_shape=tuple((ja...]
    convert_element_type x3 -> x0, other arithmetic: 6.08 us -> none  [the longest x1 4.73 us: per_device(): (blocks[:, rows:].astype(jnp.float32) * inverse[:, :, 64:65]).astype(jnp....]
    reduce_sum x3 -> x0, other arithmetic: 3.52 us -> none  [the longest x1 1.19 us: per_device(): jnp.mean(d_normed, axis=-1, keepdims=True)]
    reduce_max x2 -> x0, other arithmetic: 3.21 us -> none  [per_device(): jnp.max(jnp.abs(b.astype(jnp.float32)))]
  transfers between devices with their start and end apart: 4 -> 18, of which waited for: 3 -> 12; matrix products, arithmetic and copies ran while one was open for 6% -> 4% of each run, Pallas kernels for 0% -> 0%
where the time goes in v3:
time: 224 us
  starting transfers between devices  69.5 us (31%)
  waiting for transfers between devices  68.8 us (31%)
  blocking collectives  35.1 us (16%)
  Pallas kernels  19 us (8%)
  between operations  14.4 us (6%)
  local copies, waits for them, and re-layouts  10.4 us (5%)
  matrix products  3.72 us (2%)
  other arithmetic  2.65 us (1%)
    ppermute x16, starting transfers between devices, shifted(): lax.ppermute(array, axis, [(i, (i + by) % peers) for i in range(peers)])  69.4 us
    ppermute x16, waiting for transfers between devices, shifted(): lax.ppermute(array, axis, [(i, (i + by) % peers) for i in range(peers)])  38.5 us
    reduce_scatter x1, waiting for transfers between devices, per_device(): d_normed = lax.psum_scatter(term, 'tensor', scatter_dimension=0, tiled=True)  30.2 us
    all_to_all x1, blocking collectives, per_device(): terms = lax.all_to_all(gradients, 'dp', 0, 0)  18.1 us
    all_to_all x1, blocking collectives, per_device(): lax.all_to_all(jnp.broadcast_to(total[None], terms.shape), 'dp', 0, 0)  17.1 us
    pallas_call x1, Pallas kernels, head_backward(): pl.pallas_call(functools.partial(head_kernel, peers), out_shape=tuple((ja...  14.8 us
    unnamed x27, local copies, waits for them, and re-layouts  7.21 us
  transfers between devices with their start and end apart: 18, of which 12 were waited for; matrix products, arithmetic and copies ran while one was open for 4% of the time, Pallas kernels for 0%

profile of v3, /device:TPU:1, one launch (start us, length us, event | category | flops | bytes accessed | tf_op | source)
XLA Modules:
  0.0 223.5 jit_solution(14318895352479474463)
XLA Ops:
  7.2 2.0 shard_map.94.rest_0_
  9.2 4.4 %collective-permute-start.7 = (bf16[128,1536]{1,0:T(8,128)(2,1)}, bf16[128,1536]{1,0:T(8,128)(2,1)S(1)}, u32[]{:S(2)}, u32[]{:S(2)}) collective-permute-start(bf16[128,1536]{1,0:T(8,128)(2,1)} %shard_map.94.rest_0_), channel_id=1, source_target_pairs={{0,1},{1,2},{2,3},{3,4},{4,5},{5,6},{6,7},{7,8},{8,9},{9,10},{10,1... | collective-permute-start | bytes 1179656 | tf_op jit(solution)/shard_map/ppermute | solution.py:16
  13.6 9.5 %collective-permute-start = (bf16[128,1536]{1,0:T(8,128)(2,1)}, bf16[128,1536]{1,0:T(8,128)(2,1)S(1)}, u32[]{:S(2)}, u32[]{:S(2)}) collective-permute-start(bf16[128,1536]{1,0:T(8,128)(2,1)} %shard_map.94.rest_0_), channel_id=1, source_target_pairs={{0,15},{1,0},{2,1},{3,2},{4,3},{5,4},{6,5},{7,6},{8,7},{9,8},{10,9... | collective-permute-start | bytes 1179656 | tf_op jit(solution)/shard_map/ppermute | solution.py:16
  23.9 6.3 %collective-permute-done.7.rest_15_ = bf16[128,1536]{1,0:T(8,128)(2,1)S(1)} collective-permute-done((bf16[128,1536]{1,0:T(8,128)(2,1)}, bf16[128,1536]{1,0:T(8,128)(2,1)S(1)}, u32[]{:S(2)}, u32[]{:S(2)}) %collective-permute-start.7) | collective-permute-done | bytes 393248 | tf_op jit(solution)/shard_map/ppermute | solution.py:16
  30.2 1.9 collective-permute-start.8
  33.8 4.6 %collective-permute-start.1 = (bf16[128,1536]{1,0:T(8,128)(2,1)S(1)}, bf16[128,1536]{1,0:T(8,128)(2,1)S(1)}, u32[]{:S(2)}, u32[]{:S(2)}) collective-permute-start(bf16[128,1536]{1,0:T(8,128)(2,1)S(1)} %collective-permute-done.rest_1_), channel_id=1, source_target_pairs={{0,15},{1,0},{2,1},{3,2},{4,3},{5,4},{6,5},{7,6},{8,7},{9,8},{10,9... | collective-permute-start | bytes 1179656 | tf_op jit(solution)/shard_map/ppermute | solution.py:16
  38.4 4.3 %collective-permute-done.8.rest_14_ = bf16[128,1536]{1,0:T(8,128)(2,1)S(1)} collective-permute-done((bf16[128,1536]{1,0:T(8,128)(2,1)S(1)}, bf16[128,1536]{1,0:T(8,128)(2,1)S(1)}, u32[]{:S(2)}, u32[]{:S(2)}) %collective-permute-start.8) | collective-permute-done | bytes 393248 | tf_op jit(solution)/shard_map/ppermute | solution.py:16
  42.7 1.9 collective-permute-start.9
  45.3 5.3 %collective-permute-start.2 = (bf16[128,1536]{1,0:T(8,128)(2,1)S(1)}, bf16[128,1536]{1,0:T(8,128)(2,1)S(1)}, u32[]{:S(2)}, u32[]{:S(2)}) collective-permute-start(bf16[128,1536]{1,0:T(8,128)(2,1)S(1)} %collective-permute-done.1.rest_2_), channel_id=1, source_target_pairs={{0,15},{1,0},{2,1},{3,2},{4,3},{5,4},{6,5},{7,6},{8,7},{9,8},{10,9... | collective-permute-start | bytes 1179656 | tf_op jit(solution)/shard_map/ppermute | solution.py:16
  50.6 3.7 %collective-permute-done.9.rest_13_ = bf16[128,1536]{1,0:T(8,128)(2,1)S(1)} collective-permute-done((bf16[128,1536]{1,0:T(8,128)(2,1)S(1)}, bf16[128,1536]{1,0:T(8,128)(2,1)S(1)}, u32[]{:S(2)}, u32[]{:S(2)}) %collective-permute-start.9) | collective-permute-done | bytes 393248 | tf_op jit(solution)/shard_map/ppermute | solution.py:16
  54.4 1.9 collective-permute-start.10
  56.6 5.3 %collective-permute-start.3 = (bf16[128,1536]{1,0:T(8,128)(2,1)S(1)}, bf16[128,1536]{1,0:T(8,128)(2,1)S(1)}, u32[]{:S(2)}, u32[]{:S(2)}) collective-permute-start(bf16[128,1536]{1,0:T(8,128)(2,1)S(1)} %collective-permute-done.2.rest_3_), channel_id=1, source_target_pairs={{0,15},{1,0},{2,1},{3,2},{4,3},{5,4},{6,5},{7,6},{8,7},{9,8},{10,9... | collective-permute-start | bytes 1179656 | tf_op jit(solution)/shard_map/ppermute | solution.py:16
  61.9 3.2 %collective-permute-done.10.rest_12_ = bf16[128,1536]{1,0:T(8,128)(2,1)S(1)} collective-permute-done((bf16[128,1536]{1,0:T(8,128)(2,1)S(1)}, bf16[128,1536]{1,0:T(8,128)(2,1)S(1)}, u32[]{:S(2)}, u32[]{:S(2)}) %collective-permute-start.10) | collective-permute-done | bytes 393248 | tf_op jit(solution)/shard_map/ppermute | solution.py:16
  65.1 1.9 collective-permute-start.11
  67.0 5.3 %collective-permute-start.4 = (bf16[128,1536]{1,0:T(8,128)(2,1)S(1)}, bf16[128,1536]{1,0:T(8,128)(2,1)S(1)}, u32[]{:S(2)}, u32[]{:S(2)}) collective-permute-start(bf16[128,1536]{1,0:T(8,128)(2,1)S(1)} %collective-permute-done.3.rest_4_), channel_id=1, source_target_pairs={{0,15},{1,0},{2,1},{3,2},{4,3},{5,4},{6,5},{7,6},{8,7},{9,8},{10,9... | collective-permute-start | bytes 1179656 | tf_op jit(solution)/shard_map/ppermute | solution.py:16
  72.3 2.9 %collective-permute-done.11.rest_11_ = bf16[128,1536]{1,0:T(8,128)(2,1)S(1)} collective-permute-done((bf16[128,1536]{1,0:T(8,128)(2,1)S(1)}, bf16[128,1536]{1,0:T(8,128)(2,1)S(1)}, u32[]{:S(2)}, u32[]{:S(2)}) %collective-permute-start.11) | collective-permute-done | bytes 393248 | tf_op jit(solution)/shard_map/ppermute | solution.py:16
  75.2 1.9 collective-permute-start.12
  77.1 5.3 %collective-permute-start.5 = (bf16[128,1536]{1,0:T(8,128)(2,1)S(1)}, bf16[128,1536]{1,0:T(8,128)(2,1)}, u32[]{:S(2)}, u32[]{:S(2)}) collective-permute-start(bf16[128,1536]{1,0:T(8,128)(2,1)S(1)} %collective-permute-done.4.rest_5_), channel_id=1, source_target_pairs={{0,15},{1,0},{2,1},{3,2},{4,3},{5,4},{6,5},{7,6},{8,7},{9,8},{10,9... | collective-permute-start | bytes 1179656 | tf_op jit(solution)/shard_map/ppermute | solution.py:16
  84.9 1.9 collective-permute-start.13
  87.6 4.7 %collective-permute-start.6 = (bf16[128,1536]{1,0:T(8,128)(2,1)}, bf16[128,1536]{1,0:T(8,128)(2,1)}, u32[]{:S(2)}, u32[]{:S(2)}) collective-permute-start(bf16[128,1536]{1,0:T(8,128)(2,1)} %collective-permute-done.5.rest_6_), channel_id=1, source_target_pairs={{0,15},{1,0},{2,1},{3,2},{4,3},{5,4},{6,5},{7,6},{8,7},{9,8},{10,9... | collective-permute-start | bytes 1179656 | tf_op jit(solution)/shard_map/ppermute | solution.py:16
  92.3 2.5 %collective-permute-done.13.rest_9_ = bf16[128,1536]{1,0:T(8,128)(2,1)} collective-permute-done((bf16[128,1536]{1,0:T(8,128)(2,1)S(1)}, bf16[128,1536]{1,0:T(8,128)(2,1)}, u32[]{:S(2)}, u32[]{:S(2)}) %collective-permute-start.13) | collective-permute-done | bytes 393248 | tf_op jit(solution)/shard_map/ppermute | solution.py:16
  94.8 1.9 collective-permute-start.14
  97.7 7.5 %collective-permute-done.14.rest_8_ = bf16[128,1536]{1,0:T(8,128)(2,1)} collective-permute-done((bf16[128,1536]{1,0:T(8,128)(2,1)}, bf16[128,1536]{1,0:T(8,128)(2,1)}, u32[]{:S(2)}, u32[]{:S(2)}) %collective-permute-start.14) | collective-permute-done | bytes 393248 | tf_op jit(solution)/shard_map/ppermute | solution.py:16
  108.2 14.8 %shard_map.95 = (bf16[1024,1536]{1,0:T(8,128)(2,1)}, bf16[1024,384]{1,0:T(8,128)(2,1)}, bf16[1024,128]{1,0:T(8,128)(2,1)S(1)}, bf16[1024,1536]{1,0:T(8,128)(2,1)}, bf16[1024,1536]{1,0:T(8,128)(2,1)}) custom-call(s32[1,1]{1,0:T(1,128)} %bitcast.2.where, bf16[8,256,384]{2,1,0:T(8,128)(2,1)} %bitcast.54, s32[1024,1]{1,0:T(8,128)} %copy.10.seg_col, ...), custom_call_target="tpu_custom_call" | custom-call | flops 5000000000 | bytes 12000000 | tf_op jit(solution)/shard_map/pallas_call | solution.py:158
  123.1 1.9 copy-done.10
  125.0 3.1 %convolution_convert_fusion = bf16[1536,384]{1,0:T(8,128)(2,1)S(1)} fusion(bf16[1024,1536]{1,0:T(8,128)(2,1)S(1)} %copy-done.10, bf16[1024,384]{1,0:T(8,128)(2,1)} %get-tuple-element.10), kind=kOutput, calls=%fused_computation | convolution fusion | flops 1208549376 | bytes 5111808 | tf_op jit(solution)/shard_map/dot_general | solution.py:20
  129.0 18.1 %all_to_all.10 = bf16[8,256,384]{2,1,0:T(8,128)(2,1)S(1)} all-to-all(bf16[8,256,384]{2,1,0:T(8,128)(2,1)S(1)} %constant_dynamic-update-slice_fusion), channel_id=1, replica_groups=mesh['dp'=8,'pipe'=4,'tensor'=16] {'dp'}, dimensions={0} | all-to-all | bytes 3145728 | tf_op jit(solution)/shard_map/all_to_all | solution.py:204
  147.5 17.1 %all_to_all.11 = bf16[8,256,384]{2,1,0:T(8,128)(2,1)S(1)} all-to-all(bf16[8,256,384]{2,1,0:T(8,128)(2,1)S(1)} %broadcast_in_dim.13), channel_id=1, replica_groups=mesh['dp'=8,'pipe'=4,'tensor'=16] {'dp'}, dimensions={0} | all-to-all | bytes 3145728 | tf_op jit(solution)/shard_map/all_to_all | solution.py:206
  165.7 30.2 %reduce-scatter.2.cloned.1.call-done.d_normed = bf16[64,1536]{1,0:T(8,128)(2,1)} async-done(((bf16[1024,1536]{1,0:T(8,128)(2,1)}), bf16[64,1536]{1,0:T(8,128)(2,1)}) %reduce-scatter.2.cloned.1.call-update) | async-done | bytes 196624 | tf_op jit(solution)/shard_map/reduce_scatter | solution.py:198
  195.9 2.2 shard_map.96
  198.0 11.7 %collective-permute-start.15 = (bf16[64,1536]{1,0:T(8,128)(2,1)}, bf16[64,1536]{1,0:T(8,128)(2,1)S(1)}, u32[]{:S(2)}, u32[]{:S(2)}) collective-permute-start(bf16[64,1536]{1,0:T(8,128)(2,1)} %shard_map.96), channel_id=1, source_target_pairs={{0,48},{16,0},{32,16},{48,32},{1,49},{17,1},{33,17},{49,33},{2,50}... | collective-permute-start | bytes 589832 | tf_op jit(solution)/shard_map/ppermute | solution.py:16
  210.6 5.4 %collective-permute-done.15 = bf16[64,1536]{1,0:T(8,128)(2,1)S(1)} collective-permute-done((bf16[64,1536]{1,0:T(8,128)(2,1)}, bf16[64,1536]{1,0:T(8,128)(2,1)S(1)}, u32[]{:S(2)}, u32[]{:S(2)}) %collective-permute-start.15) | collective-permute-done | bytes 196640 | tf_op jit(solution)/shard_map/ppermute | solution.py:16
  (51 shorter events, 14.6 us)
Async XLA Ops:
  7.2 89.5 %copy-start.1 = (s32[1,1,1024]{2,1,0:T(1,128)S(1)}, s32[1,1,1024]{2,1,0:T(1,128)}, u32[]{:S(2)}) copy-start(s32[1,1,1024]{2,1,0:T(1,128)} %param.9) | copy-start | bytes 12292
  7.2 98.1 %copy-start.7 = (f32[1,128]{1,0:T(1,128)S(1)}, f32[1,128]{1,0:T(1,128)}, u32[]{:S(2)}) copy-start(f32[1,128]{1,0:T(1,128)} %k_gain.1) | copy-start | bytes 1540
  7.2 98.0 %copy-start.6 = (f32[1,128]{1,0:T(1,128)S(1)}, f32[1,128]{1,0:T(1,128)}, u32[]{:S(2)}) copy-start(f32[1,128]{1,0:T(1,128)} %q_gain.1) | copy-start | bytes 1540
  7.2 90.5 %all-gather.3.cloned.1.call-start = ((), (), s32[]{:S(2)}) async-start(), calls=%async_computation.4 | async-start | bytes 1769472 | tf_op jit(solution)/shard_map/all_gather | solution.py:187
  9.2 21.0 %collective-permute-start.7 = (bf16[128,1536]{1,0:T(8,128)(2,1)}, bf16[128,1536]{1,0:T(8,128)(2,1)S(1)}, u32[]{:S(2)}, u32[]{:S(2)}) collective-permute-start(bf16[128,1536]{1,0:T(8,128)(2,1)} %shard_map.94.rest_0_), channel_id=1, source_target_pairs={{0,1},{1,2},{2,3},{3,4},{4,5},{5,6},{6,7},{7,8},{8,9},{9,10},{10,1... | collective-permute-start | bytes 1179656 | tf_op jit(solution)/shard_map/ppermute | solution.py:16
  13.6 20.2 %collective-permute-start = (bf16[128,1536]{1,0:T(8,128)(2,1)}, bf16[128,1536]{1,0:T(8,128)(2,1)S(1)}, u32[]{:S(2)}, u32[]{:S(2)}) collective-permute-start(bf16[128,1536]{1,0:T(8,128)(2,1)} %shard_map.94.rest_0_), channel_id=1, source_target_pairs={{0,15},{1,0},{2,1},{3,2},{4,3},{5,4},{6,5},{7,6},{8,7},{9,8},{10,9... | collective-permute-start | bytes 1179656 | tf_op jit(solution)/shard_map/ppermute | solution.py:16
  30.2 8.2 %copy-start.9 = (bf16[128,1536]{1,0:T(8,128)(2,1)}, bf16[128,1536]{1,0:T(8,128)(2,1)S(1)}, u32[]{:S(2)}) copy-start(bf16[128,1536]{1,0:T(8,128)(2,1)S(1)} %collective-permute-done.7.rest_15_) | copy-start | bytes 1179652
  30.2 12.5 %collective-permute-start.8 = (bf16[128,1536]{1,0:T(8,128)(2,1)S(1)}, bf16[128,1536]{1,0:T(8,128)(2,1)S(1)}, u32[]{:S(2)}, u32[]{:S(2)}) collective-permute-start(bf16[128,1536]{1,0:T(8,128)(2,1)S(1)} %collective-permute-done.7.rest_15_), channel_id=1, source_target_pairs={{0,1},{1,2},{2,3},{3,4},{4,5},{5,6},{6,7},{7,8},{8,9},{9,10},{10,1... | collective-permute-start | bytes 1179656 | tf_op jit(solution)/shard_map/ppermute | solution.py:16
  33.8 162.1 %reduce-scatter.2.cloned.1.call-start = ((), (), s32[]{:S(2)}) async-start(), calls=%async_computation.3 | async-start | bytes 3342336 | tf_op jit(solution)/shard_map/reduce_scatter | solution.py:198
  33.8 11.5 %collective-permute-start.1 = (bf16[128,1536]{1,0:T(8,128)(2,1)S(1)}, bf16[128,1536]{1,0:T(8,128)(2,1)S(1)}, u32[]{:S(2)}, u32[]{:S(2)}) collective-permute-start(bf16[128,1536]{1,0:T(8,128)(2,1)S(1)} %collective-permute-done.rest_1_), channel_id=1, source_target_pairs={{0,15},{1,0},{2,1},{3,2},{4,3},{5,4},{6,5},{7,6},{8,7},{9,8},{10,9... | collective-permute-start | bytes 1179656 | tf_op jit(solution)/shard_map/ppermute | solution.py:16
  42.7 11.7 %collective-permute-start.9 = (bf16[128,1536]{1,0:T(8,128)(2,1)S(1)}, bf16[128,1536]{1,0:T(8,128)(2,1)S(1)}, u32[]{:S(2)}, u32[]{:S(2)}) collective-permute-start(bf16[128,1536]{1,0:T(8,128)(2,1)S(1)} %collective-permute-done.8.rest_14_), channel_id=1, source_target_pairs={{0,1},{1,2},{2,3},{3,4},{4,5},{5,6},{6,7},{7,8},{8,9},{9,10},{10,1... | collective-permute-start | bytes 1179656 | tf_op jit(solution)/shard_map/ppermute | solution.py:16
  45.3 11.3 %collective-permute-start.2 = (bf16[128,1536]{1,0:T(8,128)(2,1)S(1)}, bf16[128,1536]{1,0:T(8,128)(2,1)S(1)}, u32[]{:S(2)}, u32[]{:S(2)}) collective-permute-start(bf16[128,1536]{1,0:T(8,128)(2,1)S(1)} %collective-permute-done.1.rest_2_), channel_id=1, source_target_pairs={{0,15},{1,0},{2,1},{3,2},{4,3},{5,4},{6,5},{7,6},{8,7},{9,8},{10,9... | collective-permute-start | bytes 1179656 | tf_op jit(solution)/shard_map/ppermute | solution.py:16
  54.4 10.7 %collective-permute-start.10 = (bf16[128,1536]{1,0:T(8,128)(2,1)S(1)}, bf16[128,1536]{1,0:T(8,128)(2,1)S(1)}, u32[]{:S(2)}, u32[]{:S(2)}) collective-permute-start(bf16[128,1536]{1,0:T(8,128)(2,1)S(1)} %collective-permute-done.9.rest_13_), channel_id=1, source_target_pairs={{0,1},{1,2},{2,3},{3,4},{4,5},{5,6},{6,7},{7,8},{8,9},{9,10},{10,1... | collective-permute-start | bytes 1179656 | tf_op jit(solution)/shard_map/ppermute | solution.py:16
  56.6 10.4 %collective-permute-start.3 = (bf16[128,1536]{1,0:T(8,128)(2,1)S(1)}, bf16[128,1536]{1,0:T(8,128)(2,1)S(1)}, u32[]{:S(2)}, u32[]{:S(2)}) collective-permute-start(bf16[128,1536]{1,0:T(8,128)(2,1)S(1)} %collective-permute-done.2.rest_3_), channel_id=1, source_target_pairs={{0,15},{1,0},{2,1},{3,2},{4,3},{5,4},{6,5},{7,6},{8,7},{9,8},{10,9... | collective-permute-start | bytes 1179656 | tf_op jit(solution)/shard_map/ppermute | solution.py:16
  65.1 10.1 %collective-permute-start.11 = (bf16[128,1536]{1,0:T(8,128)(2,1)S(1)}, bf16[128,1536]{1,0:T(8,128)(2,1)S(1)}, u32[]{:S(2)}, u32[]{:S(2)}) collective-permute-start(bf16[128,1536]{1,0:T(8,128)(2,1)S(1)} %collective-permute-done.10.rest_12_), channel_id=1, source_target_pairs={{0,1},{1,2},{2,3},{3,4},{4,5},{5,6},{6,7},{7,8},{8,9},{9,10},{10,1... | collective-permute-start | bytes 1179656 | tf_op jit(solution)/shard_map/ppermute | solution.py:16
  67.0 10.1 %collective-permute-start.4 = (bf16[128,1536]{1,0:T(8,128)(2,1)S(1)}, bf16[128,1536]{1,0:T(8,128)(2,1)S(1)}, u32[]{:S(2)}, u32[]{:S(2)}) collective-permute-start(bf16[128,1536]{1,0:T(8,128)(2,1)S(1)} %collective-permute-done.3.rest_4_), channel_id=1, source_target_pairs={{0,15},{1,0},{2,1},{3,2},{4,3},{5,4},{6,5},{7,6},{8,7},{9,8},{10,9... | collective-permute-start | bytes 1179656 | tf_op jit(solution)/shard_map/ppermute | solution.py:16
  75.2 9.7 %collective-permute-start.12 = (bf16[128,1536]{1,0:T(8,128)(2,1)S(1)}, bf16[128,1536]{1,0:T(8,128)(2,1)S(1)}, u32[]{:S(2)}, u32[]{:S(2)}) collective-permute-start(bf16[128,1536]{1,0:T(8,128)(2,1)S(1)} %collective-permute-done.11.rest_11_), channel_id=1, source_target_pairs={{0,1},{1,2},{2,3},{3,4},{4,5},{5,6},{6,7},{7,8},{8,9},{9,10},{10,1... | collective-permute-start | bytes 1179656 | tf_op jit(solution)/shard_map/ppermute | solution.py:16
  77.1 10.5 %collective-permute-start.5 = (bf16[128,1536]{1,0:T(8,128)(2,1)S(1)}, bf16[128,1536]{1,0:T(8,128)(2,1)}, u32[]{:S(2)}, u32[]{:S(2)}) collective-permute-start(bf16[128,1536]{1,0:T(8,128)(2,1)S(1)} %collective-permute-done.4.rest_5_), channel_id=1, source_target_pairs={{0,15},{1,0},{2,1},{3,2},{4,3},{5,4},{6,5},{7,6},{8,7},{9,8},{10,9... | collective-permute-start | bytes 1179656 | tf_op jit(solution)/shard_map/ppermute | solution.py:16
  82.5 0.7 copy-start.2
  84.9 9.8 %collective-permute-start.13 = (bf16[128,1536]{1,0:T(8,128)(2,1)S(1)}, bf16[128,1536]{1,0:T(8,128)(2,1)}, u32[]{:S(2)}, u32[]{:S(2)}) collective-permute-start(bf16[128,1536]{1,0:T(8,128)(2,1)S(1)} %collective-permute-done.12.rest_10_), channel_id=1, source_target_pairs={{0,1},{1,2},{2,3},{3,4},{4,5},{5,6},{6,7},{7,8},{8,9},{9,10},{10,1... | collective-permute-start | bytes 1179656 | tf_op jit(solution)/shard_map/ppermute | solution.py:16
  86.9 0.8 copy-start.4
  87.6 10.1 %collective-permute-start.6 = (bf16[128,1536]{1,0:T(8,128)(2,1)}, bf16[128,1536]{1,0:T(8,128)(2,1)}, u32[]{:S(2)}, u32[]{:S(2)}) collective-permute-start(bf16[128,1536]{1,0:T(8,128)(2,1)} %collective-permute-done.5.rest_6_), channel_id=1, source_target_pairs={{0,15},{1,0},{2,1},{3,2},{4,3},{5,4},{6,5},{7,6},{8,7},{9,8},{10,9... | collective-permute-start | bytes 1179656 | tf_op jit(solution)/shard_map/ppermute | solution.py:16
  94.8 10.5 %collective-permute-start.14 = (bf16[128,1536]{1,0:T(8,128)(2,1)}, bf16[128,1536]{1,0:T(8,128)(2,1)}, u32[]{:S(2)}, u32[]{:S(2)}) collective-permute-start(bf16[128,1536]{1,0:T(8,128)(2,1)} %collective-permute-done.13.rest_9_), channel_id=1, source_target_pairs={{0,1},{1,2},{2,3},{3,4},{4,5},{5,6},{6,7},{7,8},{8,9},{9,10},{10,1... | collective-permute-start | bytes 1179656 | tf_op jit(solution)/shard_map/ppermute | solution.py:16
  105.2 1.0 copy-start
  106.2 1.0 copy-start.3
  107.2 1.0 copy-start.5
  123.1 1.9 copy-start.10
  125.0 3.3 %copy-start.8 = (bf16[1024,1536]{1,0:T(8,128)(2,1)S(1)}, bf16[1024,1536]{1,0:T(8,128)(2,1)}, u32[]{:S(2)}) copy-start(bf16[1024,1536]{1,0:T(8,128)(2,1)} %get-tuple-element.12) | copy-start | bytes 9437188
  198.0 18.0 %collective-permute-start.15 = (bf16[64,1536]{1,0:T(8,128)(2,1)}, bf16[64,1536]{1,0:T(8,128)(2,1)S(1)}, u32[]{:S(2)}, u32[]{:S(2)}) collective-permute-start(bf16[64,1536]{1,0:T(8,128)(2,1)} %shard_map.96), channel_id=1, source_target_pairs={{0,48},{16,0},{32,16},{48,32},{1,49},{17,1},{33,17},{49,33},{2,50}... | collective-permute-start | bytes 589832 | tf_op jit(solution)/shard_map/ppermute | solution.py:16
Sparse Core Ops, SparseCore 0:
  33.9 41.0 all-gather.2
  123.2 72.6 reduce-scatter.1

commit v4 on v3

--- a/solution.py
+++ b/solution.py
@@ -1,5 +1,3 @@
-import functools
-
 import jax
 import jax.numpy as jnp
 from jax import lax
@@ -9,6 +7,9 @@
 
 EPS = 1e-06
 BLOCK = 256
+TOP = 30000.0
+LEAST = 1e-30
+NOTE = 8
 
 
 def shifted(array, axis, by):
@@ -20,19 +21,6 @@
     return lax.dot_general(
         left, right, (((left_dim,), (right_dim,)), ((), ())), preferred_element_type=jnp.float32
     )
-
-
-def ring_gather(block, axis):
-    peers = lax.axis_size(axis)
-    got = {0: block}
-    up = down = block
-    for step in range(1, peers // 2 + 1):
-        up = shifted(up, axis, 1)
-        got[peers - step] = up
-        if step < peers - step:
-            down = shifted(down, axis, -1)
-            got[step] = down
-    return [got[i] for i in range(peers)]
 
 
 def fold_wide(wide, parts, width):
@@ -55,10 +43,20 @@
     return centred * rate, rate
 
 
-def first_kernel(tokens, cot, block):
-    rows = tokens.shape[0]
-    block[0:rows, :] = normalised(tokens[...])[0].astype(jnp.bfloat16)
-    block[rows:, :] = cot[...]
+def first_kernel(tokens, cot, w_in, w_out, block, weights):
+    rows, columns = tokens.shape
+    share, three = w_in.shape
+    weights[0:share, :] = w_in[...]
+    for c in range(columns // three):
+        low = share + c * w_out.shape[0]
+        weights[low : low + w_out.shape[0], :] = w_out[:, c * three : (c + 1) * three]
+    halves = (normalised(tokens[...])[0].astype(jnp.bfloat16).astype(jnp.float32), cot[...].astype(jnp.float32))
+    for at, half in enumerate(halves):
+        most = jnp.max(jnp.max(jnp.abs(half), axis=1, keepdims=True), axis=0, keepdims=True)
+        power = jnp.floor(jnp.log2(TOP / jnp.maximum(most, LEAST)))
+        block[at * rows : (at + 1) * rows, :] = half * jnp.exp2(power)
+        wide = columns // 2
+        block[2 * rows :, at * wide : (at + 1) * wide] = jnp.broadcast_to(power, (NOTE, wide))
 
 
 def last_kernel(tokens, cot, d_normed, out):
@@ -68,11 +66,12 @@
     out[...] = (cot[...].astype(jnp.float32) + rate * inner).astype(jnp.bfloat16)
 
 
-def head_kernel(peers, where, weights, seg_col, seg_row, q_gain, k_gain, *rest):
-    blocks, rest = rest[:peers], rest[peers:]
-    term, d_joined, attended, normed, cot = rest[:5]
-    (proj, outw, made, sems,
-     q_unit, k_unit, q_rate, k_rate, q_norm, k_norm, v_low, d_att, d_key, d_val) = rest[5:]
+def head_kernel(
+    normed, cot, weights, seg_col, seg_row, q_gain, k_gain,
+    term, d_joined, attended,
+    proj, outw, made, sems,
+    q_unit, k_unit, q_rate, k_rate, q_norm, k_norm, v_low, d_att, d_key, d_val,
+):
     tokens, width = q_norm.shape
     share = proj.shape[0] // weights.shape[0]
     three = proj.shape[1]
@@ -82,12 +81,6 @@
         for c in range(outw.shape[1] // three):
             low = share + c * piece
             outw[p * piece : (p + 1) * piece, c * three : (c + 1) * three] = weights[p, low : low + piece, :]
-    each = tokens // peers
-    for d in range(peers):
-        at = lax.rem(where[0, 0] + d, peers) * each
-        at = pl.multiple_of(at, each)
-        normed[pl.ds(at, each), :] = blocks[d][0:each, :]
-        cot[pl.ds(at, each), :] = blocks[d][each:, :]
     factor = width ** (-0.5)
     count = tokens // BLOCK
     for i in range(count):
@@ -144,10 +137,8 @@
         copy.wait()
 
 
-def head_backward(blocks, weights, share, segments, q_scale, k_scale, me):
-    peers = len(blocks)
-    tokens = segments.shape[0]
-    features = blocks[0].shape[1]
+def head_backward(normed, cotangent, weights, segments, q_scale, k_scale):
+    tokens, features = normed.shape
     width = q_scale.shape[0]
     here = pl.BlockSpec(memory_space=pltpu.VMEM)
     low = jnp.bfloat16
@@ -156,12 +147,12 @@
         return pltpu.VMEM((tokens, columns), dtype)
 
     return pl.pallas_call(
-        functools.partial(head_kernel, peers),
+        head_kernel,
         out_shape=tuple(
-            jax.ShapeDtypeStruct((tokens, columns), low) for columns in (features, 3 * width, width, features, features)
+            jax.ShapeDtypeStruct((tokens, columns), low) for columns in (features, 3 * width, width)
         ),
-        in_specs=[pl.BlockSpec(memory_space=pltpu.SMEM)] + [here] * (5 + peers),
-        out_specs=(pl.BlockSpec(memory_space=pl.ANY),) + (here,) * 4,
+        in_specs=[here] * 7,
+        out_specs=(pl.BlockSpec(memory_space=pl.ANY), here, here),
         scratch_shapes=[
             pltpu.VMEM((features, 3 * width), low), pltpu.VMEM((width, features), low), kept(features, low),
             pltpu.SemaphoreType.DMA((tokens // BLOCK,)),
@@ -172,28 +163,37 @@
         compiler_params=pltpu.CompilerParams(vmem_limit_bytes=48 * 1024 * 1024),
         cost_estimate=pl.CostEstimate(flops=5_000_000_000, bytes_accessed=12_000_000, transcendentals=1_000_000),
     )(
-        me.reshape(1, 1), weights, segments[:, None], segments[None, :], q_scale[None, :], k_scale[None, :], *blocks
+        normed, cotangent, weights, segments[:, None], segments[None, :], q_scale[None, :], k_scale[None, :]
     )
 
 
 def per_device(saved_input, grad_in, segment_ids, w_qkv, w_out, q_gain, k_gain):
     dp = lax.axis_size("dp")
-    me = lax.axis_index("tensor").astype(jnp.int32)
     tokens, cot = saved_input[0, 0], grad_in[0, 0]
     three = w_qkv.shape[3]
     share = w_qkv.shape[1]
     here = pl.BlockSpec(memory_space=pltpu.VMEM)
-    weights = jnp.concatenate([w_qkv[0, :, 0, :], fold_wide(w_out[0, 0], 1, three)[0]], axis=0)
+    rows, features = tokens.shape
+    block, weights = pl.pallas_call(
+        first_kernel,
+        out_shape=(
+            jax.ShapeDtypeStruct((2 * rows + NOTE, features), jnp.float32),
+            jax.ShapeDtypeStruct((share + w_out.shape[2] * features // three, three), jnp.bfloat16),
+        ),
+        in_specs=[here] * 4,
+        out_specs=(here, here),
+    )(tokens, cot, w_qkv[0, :, 0, :], w_out[0, 0])
     weights = lax.all_gather(weights, "dp", axis=0)
-    block = pl.pallas_call(
-        first_kernel,
-        out_shape=jax.ShapeDtypeStruct((2 * tokens.shape[0], tokens.shape[1]), jnp.bfloat16),
-        in_specs=[here, here],
-        out_specs=here,
-    )(tokens, cot)
-    blocks = ring_gather(block, "tensor")
-    term, d_joined, attended, normed, cotangent = head_backward(
-        blocks, weights, share, segment_ids[0, 0], q_gain[0], k_gain[0], me
+    blocks = lax.all_gather(block.astype(jnp.float16), "tensor", axis=0)
+    powers = blocks[:, 2 * rows : 2 * rows + 1, :].astype(jnp.float32)
+    halves = (
+        blocks[:, at * rows : (at + 1) * rows].astype(jnp.float32)
+        * jnp.exp2(-powers[:, :, at * features // 2 : at * features // 2 + 1])
+        for at in (0, 1)
+    )
+    normed, cotangent = (half.astype(jnp.bfloat16).reshape(-1, features) for half in halves)
+    term, d_joined, attended = head_backward(
+        normed, cotangent, weights, segment_ids[0, 0], q_gain[0], k_gain[0]
     )
     d_normed = lax.psum_scatter(term, "tensor", scatter_dimension=0, tiled=True)
     d_outw = contract(attended, cotangent, 0, 0)

time: 224 us -> 213 us (0.951)
  blocking collectives: 35.1 us -> 120 us
  starting transfers between devices: 69.5 us -> 11.6 us
  waiting for transfers between devices: 68.8 us -> 30.4 us
  other arithmetic: 2.65 us -> 7.6 us
  local copies, waits for them, and re-layouts: 10.4 us -> 7.11 us
    all_gather x0 -> x1, blocking collectives: none -> 82.7 us  [per_device(): blocks = lax.all_gather(block.astype(jnp.float16), 'tensor', axis=0)]
    ppermute x16 -> x1, starting transfers between devices: 69.4 us -> 11.6 us  [shifted(): lax.ppermute(array, axis, [(i, (i + by) % peers) for i in range(peers)])]
    ppermute x16 -> x1, waiting for transfers between devices: 38.5 us -> 5.53 us  [shifted(): lax.ppermute(array, axis, [(i, (i + by) % peers) for i in range(peers)])]
    convert_element_type x0 -> x3, other arithmetic: none -> 6.56 us  [the longest x1 5.31 us: per_device(): half.astype(jnp.bfloat16).reshape(-1, features)]
    reduce_scatter x1, waiting for transfers between devices: 30.2 us -> 24.8 us  [per_device(): d_normed = lax.psum_scatter(term, 'tensor', scatter_dimension=0, tiled=True)]
    all_to_all x1, blocking collectives: 18.1 us -> 20.5 us  [per_device(): terms = lax.all_to_all(gradients, 'dp', 0, 0)]
    unnamed x27 -> x18, local copies, waits for them, and re-layouts: 7.21 us -> 5.44 us
  transfers between devices with their start and end apart: 18 -> 3, of which waited for: 12 -> 2; matrix products, arithmetic and copies ran while one was open for 4% -> 7% of each run, Pallas kernels for 0% -> 0%
where the time goes in v4:
time: 213 us
  blocking collectives  120 us (56%)
  waiting for transfers between devices  30.4 us (14%)
  Pallas kernels  16.9 us (8%)
  between operations  14.2 us (7%)
  starting transfers between devices  11.6 us (5%)
  other arithmetic  7.6 us (4%)
  local copies, waits for them, and re-layouts  7.11 us (3%)
  matrix products  4.48 us (2%)
    all_gather x1, blocking collectives, per_device(): blocks = lax.all_gather(block.astype(jnp.float16), 'tensor', axis=0)  82.7 us
    reduce_scatter x1, waiting for transfers between devices, per_device(): d_normed = lax.psum_scatter(term, 'tensor', scatter_dimension=0, tiled=True)  24.8 us
    all_to_all x1, blocking collectives, per_device(): terms = lax.all_to_all(gradients, 'dp', 0, 0)  20.5 us
    all_to_all x1, blocking collectives, per_device(): lax.all_to_all(jnp.broadcast_to(total[None], terms.shape), 'dp', 0, 0)  17.3 us
    pallas_call x1, Pallas kernels, head_backward(): pl.pallas_call(head_kernel, out_shape=tuple((jax.ShapeDtypeStruct((tokens...  12.3 us
    ppermute x1, starting transfers between devices, shifted(): lax.ppermute(array, axis, [(i, (i + by) % peers) for i in range(peers)])  11.6 us
    ppermute x1, waiting for transfers between devices, shifted(): lax.ppermute(array, axis, [(i, (i + by) % peers) for i in range(peers)])  5.53 us
    unnamed x18, local copies, waits for them, and re-layouts  5.44 us
  transfers between devices with their start and end apart: 3, of which 2 were waited for; matrix products, arithmetic and copies ran while one was open for 7% of the time, Pallas kernels for 0%

profile of v4, /device:TPU:1, one launch (start us, length us, event | category | flops | bytes accessed | tf_op | source)
XLA Modules:
  0.0 212.8 jit_solution(8326351421827838683)
XLA Ops:
  7.2 0.0 all-gather.5.cloned.1.call-start
  7.2 2.4 %shard_map.94 = (f32[136,1536]{1,0:T(8,128)}, bf16[256,384]{1,0:T(8,128)(2,1)}) custom-call(bf16[64,1536]{1,0:T(8,128)(2,1)} %bitcast.42, bf16[64,1536]{1,0:T(8,128)(2,1)} %bitcast.44, bf16[192,384]{1,0:T(8,128)(2,1)} %bitcast.55, bf16[16,1536]{1,0:T(8,128)(2,1)} %bitcast.56), custom_call_target="tpu_custom_call" | custom-call | tf_op jit(solution)/shard_map/pallas_call | solution.py:177
  9.6 0.0 all-gather.5.cloned.1.call-update
  9.7 0.0 reduce-scatter.2.cloned.1.call-start
  9.7 1.2 convert_element_type.26
  10.9 82.7 %all-gather.6 = f16[2176,1536]{1,0:T(8,128)(2,1)S(1)} all-gather(f16[136,1536]{1,0:T(8,128)(2,1)S(1)} %convert_element_type.26), channel_id=2, replica_groups=mesh['dp'=8,'pipe'=4,'tensor'=16] {'tensor'}, dimensions={0}, use_global_device_ids=true | all-gather | bytes 7102464 | tf_op jit(solution)/shard_map/all_gather | solution.py:187
  93.6 2.7 %copy-done.4 = f16[2176,1536]{1,0:T(8,128)(2,1)} copy-done((f16[2176,1536]{1,0:T(8,128)(2,1)}, f16[2176,1536]{1,0:T(8,128)(2,1)S(1)}, u32[]{:S(2)}) %copy-start.4) | copy-done | bytes 6684696
  96.3 0.1 slice.62
  96.4 0.4 copy.13
  96.9 0.1 convert_element_type.28
  96.9 0.2 copy.12.seg_col
  97.2 0.0 copy-start.2
  97.2 0.0 copy-start.3
  97.2 5.3 %multiply_convert_fusion = (bf16[16,64,1536]{2,1,0:T(8,128)(2,1)}, bf16[16,64,1536]{2,1,0:T(8,128)(2,1)}) fusion(f16[16,136,1536]{2,1,0:T(8,128)(2,1)} %bitcast.35, f32[16]{0:T(128)S(1)} %get-tuple-element.19, f32[16]{0:T(128)S(1)} %get-tuple-element.20), kind=kLoop, calls=%fused_computation | loop fusion | flops 9437184 | bytes 12583040 | tf_op jit(solution)/shard_map/convert_element_type | solution.py:194
  102.5 0.0 copy-done.2
  102.5 1.4 copy-done.1
  103.9 12.3 %shard_map.95 = (bf16[1024,1536]{1,0:T(8,128)(2,1)}, bf16[1024,384]{1,0:T(8,128)(2,1)S(1)}, bf16[1024,128]{1,0:T(8,128)(2,1)S(1)}) custom-call(bf16[1024,1536]{1,0:T(8,128)(2,1)} %bitcast.38, bf16[1024,1536]{1,0:T(8,128)(2,1)} %bitcast.36, bf16[8,256,384]{2,1,0:T(8,128)(2,1)S(1)} %bitcast.33, s32[1024,1]{1,0:T(8,128)S(1)} %copy.12.seg_col, ...), custom_call_target="tpu_custom_call" | custom-call | flops 5000000000 | bytes 12000000 | tf_op jit(solution)/shard_map/pallas_call | solution.py:149
  116.2 0.0 reduce-scatter.2.cloned.1.call-update
  116.3 3.9 %convolution_convert_fusion = bf16[1536,384]{1,0:T(8,128)(2,1)S(1)} fusion(bf16[1024,1536]{1,0:T(8,128)(2,1)} %bitcast.39, bf16[1024,384]{1,0:T(8,128)(2,1)S(1)} %get-tuple-element.11), kind=kOutput, calls=%fused_computation.2 | convolution fusion | flops 1208549376 | bytes 5111808 | tf_op jit(solution)/shard_map/dot_general | solution.py:21
  120.1 0.1 constant_dynamic-update-slice_fusion.4
  120.3 0.6 convolution_convert_fusion.1
  121.0 20.5 %all_to_all.10 = bf16[8,256,384]{2,1,0:T(8,128)(2,1)S(1)} all-to-all(bf16[8,256,384]{2,1,0:T(8,128)(2,1)S(1)} %constant_dynamic-update-slice_fusion), channel_id=1, replica_groups=mesh['dp'=8,'pipe'=4,'tensor'=16] {'dp'}, dimensions={0} | all-to-all | bytes 3145728 | tf_op jit(solution)/shard_map/all_to_all | solution.py:204
  141.5 0.3 reduce_sum.12
  141.8 0.1 broadcast_in_dim.13
  141.9 17.3 %all_to_all.11 = bf16[8,256,384]{2,1,0:T(8,128)(2,1)S(1)} all-to-all(bf16[8,256,384]{2,1,0:T(8,128)(2,1)S(1)} %broadcast_in_dim.13), channel_id=1, replica_groups=mesh['dp'=8,'pipe'=4,'tensor'=16] {'dp'}, dimensions={0} | all-to-all | bytes 3145728 | tf_op jit(solution)/shard_map/all_to_all | solution.py:206
  159.2 1.1 slice.70
  160.4 24.8 %reduce-scatter.2.cloned.1.call-done.d_normed = bf16[64,1536]{1,0:T(8,128)(2,1)} async-done(((bf16[1024,1536]{1,0:T(8,128)(2,1)}), bf16[64,1536]{1,0:T(8,128)(2,1)}) %reduce-scatter.2.cloned.1.call-update) | async-done | bytes 196624 | tf_op jit(solution)/shard_map/reduce_scatter | solution.py:198
  185.2 2.2 %shard_map.96 = bf16[64,1536]{1,0:T(8,128)(2,1)} custom-call(bf16[64,1536]{1,0:T(8,128)(2,1)} %bitcast.43, bf16[64,1536]{1,0:T(8,128)(2,1)} %bitcast.45, bf16[64,1536]{1,0:T(8,128)(2,1)} %reduce-scatter.2.cloned.1.call-done.d_normed), custom_call_target="tpu_custom_call" | custom-call | tf_op jit(solution)/shard_map/pallas_call | solution.py:209
  187.4 11.6 %collective-permute-start = (bf16[64,1536]{1,0:T(8,128)(2,1)}, bf16[64,1536]{1,0:T(8,128)(2,1)S(1)}, u32[]{:S(2)}, u32[]{:S(2)}) collective-permute-start(bf16[64,1536]{1,0:T(8,128)(2,1)} %shard_map.96), channel_id=1, source_target_pairs={{0,48},{16,0},{32,16},{48,32},{1,49},{17,1},{33,17},{49,33},{2,50}... | collective-permute-start | bytes 589832 | tf_op jit(solution)/shard_map/ppermute | solution.py:17
  198.9 0.8 maximum_bitcast_fusion
  199.7 5.5 %collective-permute-done = bf16[64,1536]{1,0:T(8,128)(2,1)S(1)} collective-permute-done((bf16[64,1536]{1,0:T(8,128)(2,1)}, bf16[64,1536]{1,0:T(8,128)(2,1)S(1)}, u32[]{:S(2)}, u32[]{:S(2)}) %collective-permute-start) | collective-permute-done | bytes 196640 | tf_op jit(solution)/shard_map/ppermute | solution.py:17
  205.2 0.7 copy.19
  (15 shorter events, 0.2 us)
Async XLA Ops:
  7.2 95.3 %all-gather.5.cloned.1.call-start = ((), (), s32[]{:S(2)}) async-start(), calls=%async_computation.4 | async-start | bytes 1769472 | tf_op jit(solution)/shard_map/all_gather | solution.py:186
  9.7 175.6 %reduce-scatter.2.cloned.1.call-start = ((), (), s32[]{:S(2)}) async-start(), calls=%async_computation.3 | async-start | bytes 3342336 | tf_op jit(solution)/shard_map/reduce_scatter | solution.py:198
  93.6 2.7 %copy-start.4 = (f16[2176,1536]{1,0:T(8,128)(2,1)}, f16[2176,1536]{1,0:T(8,128)(2,1)S(1)}, u32[]{:S(2)}) copy-start(f16[2176,1536]{1,0:T(8,128)(2,1)S(1)} %all-gather.6) | copy-start | bytes 20054020
  93.6 3.3 %copy-start = (s32[1,1,1024]{2,1,0:T(1,128)S(1)}, s32[1,1,1024]{2,1,0:T(1,128)}, u32[]{:S(2)}) copy-start(s32[1,1,1024]{2,1,0:T(1,128)} %param.9) | copy-start | bytes 12292
  97.2 5.3 %copy-start.2 = (f32[1,128]{1,0:T(1,128)S(1)}, f32[1,128]{1,0:T(1,128)}, u32[]{:S(2)}) copy-start(f32[1,128]{1,0:T(1,128)} %q_gain.1) | copy-start | bytes 1540
  97.2 5.3 %copy-start.3 = (f32[1,128]{1,0:T(1,128)S(1)}, f32[1,128]{1,0:T(1,128)}, u32[]{:S(2)}) copy-start(f32[1,128]{1,0:T(1,128)} %k_gain.1) | copy-start | bytes 1540
  102.5 1.4 copy-start.1
  116.2 4.0 %copy-start.5 = (bf16[16,64,1536]{2,1,0:T(8,128)(2,1)S(1)}, bf16[16,64,1536]{2,1,0:T(8,128)(2,1)}, u32[]{:S(2)}) copy-start(bf16[16,64,1536]{2,1,0:T(8,128)(2,1)} %get-tuple-element.13) | copy-start | bytes 9437188
  187.4 17.9 %collective-permute-start = (bf16[64,1536]{1,0:T(8,128)(2,1)}, bf16[64,1536]{1,0:T(8,128)(2,1)S(1)}, u32[]{:S(2)}, u32[]{:S(2)}) collective-permute-start(bf16[64,1536]{1,0:T(8,128)(2,1)} %shard_map.96), channel_id=1, source_target_pairs={{0,48},{16,0},{32,16},{48,32},{1,49},{17,1},{33,17},{49,33},{2,50}... | collective-permute-start | bytes 589832 | tf_op jit(solution)/shard_map/ppermute | solution.py:17
Sparse Core Ops, SparseCore 0:
  10.7 47.3 all-gather.4
  116.4 68.8 reduce-scatter.1

commit v5 on v4

--- a/solution.py
+++ b/solution.py
@@ -70,7 +70,7 @@
     normed, cot, weights, seg_col, seg_row, q_gain, k_gain,
     term, d_joined, attended,
     proj, outw, made, sems,
-    q_unit, k_unit, q_rate, k_rate, q_norm, k_norm, v_low, d_att, d_key, d_val,
+    q_unit, k_unit, q_rate, k_rate, q_norm, k_norm, v_low, d_att, d_key, d_val, k_turned, v_turned,
 ):
     tokens, width = q_norm.shape
     share = proj.shape[0] // weights.shape[0]
@@ -97,6 +97,8 @@
             unit[rows, :] = u
             norm[rows, :] = (u * gain[...]).astype(jnp.bfloat16)
         v_low[rows, :] = joined[:, 2 * width :].astype(jnp.bfloat16)
+        v_turned[:, rows] = joined[:, 2 * width :].T.astype(jnp.bfloat16)
+        k_turned[:, rows] = (k_unit[rows, :] * k_gain[...]).T.astype(jnp.bfloat16)
         d_att[rows, :] = contract(cot[rows, :], outw[...], 1, 1).astype(jnp.bfloat16)
     d_key[...] = jnp.zeros_like(d_key)
     d_val[...] = jnp.zeros_like(d_val)
@@ -106,19 +108,22 @@
             rows = pl.ds(i * BLOCK, BLOCK)
             low, high = max(i - 1, 0), min(i + 2, count)
             near = pl.ds(low * BLOCK, (high - low) * BLOCK)
-            qn, kn, vb, do = q_norm[rows, :], k_norm[near, :], v_low[near, :], d_att[rows, :]
-            scores = contract(qn, kn, 1, 1) * factor
-            same = seg_col[rows, :] == seg_row[:, low * BLOCK : high * BLOCK]
+            qn, do = q_norm[rows, :], d_att[rows, :]
+            scores = contract(k_norm[near, :], qn, 1, 1) * factor
+            same = seg_col[near, :] == seg_row[:, i * BLOCK : (i + 1) * BLOCK]
             expd = jnp.where(same, jnp.exp(scores), 0.0)
-            probs = expd / jnp.sum(expd, axis=-1, keepdims=True)
+            probs = expd * (1.0 / jnp.sum(expd, axis=0, keepdims=True))
             probs_low = probs.astype(jnp.bfloat16)
-            attended[rows, :] = jnp.dot(probs_low, vb, preferred_element_type=jnp.float32).astype(jnp.bfloat16)
-            d_probs = contract(do, vb, 1, 1)
-            d_val[near, :] += contract(probs_low, do, 0, 0)
-            delta = jnp.sum(probs * d_probs, axis=-1, keepdims=True)
+            attended[:, rows] = jnp.dot(
+                v_turned[:, near], probs_low, preferred_element_type=jnp.float32
+            ).astype(jnp.bfloat16)
+            d_probs = contract(v_low[near, :], do, 1, 1)
+            d_val[near, :] += jnp.dot(probs_low, do, preferred_element_type=jnp.float32)
+            delta = jnp.sum(probs * d_probs, axis=0, keepdims=True)
             d_scores = (probs * (d_probs - delta) * factor).astype(jnp.bfloat16)
-            d_key[near, :] += contract(d_scores, qn, 0, 0)
-            back = jnp.dot(d_scores, kn, preferred_element_type=jnp.float32) * q_gain[...]
+            d_key[near, :] += jnp.dot(d_scores, qn, preferred_element_type=jnp.float32)
+            turned = jnp.dot(k_turned[:, near], d_scores, preferred_element_type=jnp.float32)
+            back = turned.T * q_gain[...]
             u = q_unit[rows, :]
             d_query = q_rate[rows, :] * (back - u * jnp.mean(back * u, axis=-1, keepdims=True))
             d_joined[rows, 0:width] = d_query.astype(jnp.bfloat16)
@@ -149,7 +154,7 @@
     return pl.pallas_call(
         head_kernel,
         out_shape=tuple(
-            jax.ShapeDtypeStruct((tokens, columns), low) for columns in (features, 3 * width, width)
+            jax.ShapeDtypeStruct(shape, low) for shape in ((tokens, features), (tokens, 3 * width), (width, tokens))
         ),
         in_specs=[here] * 7,
         out_specs=(pl.BlockSpec(memory_space=pl.ANY), here, here),
@@ -159,8 +164,9 @@
             kept(width, jnp.float32), kept(width, jnp.float32), kept(1, jnp.float32), kept(1, jnp.float32),
             kept(width, low), kept(width, low), kept(width, low), kept(width, low),
             kept(width, jnp.float32), kept(width, jnp.float32),
+            pltpu.VMEM((width, tokens), low), pltpu.VMEM((width, tokens), low),
         ],
-        compiler_params=pltpu.CompilerParams(vmem_limit_bytes=48 * 1024 * 1024),
+        compiler_params=pltpu.CompilerParams(vmem_limit_bytes=28 * 1024 * 1024),
         cost_estimate=pl.CostEstimate(flops=5_000_000_000, bytes_accessed=12_000_000, transcendentals=1_000_000),
     )(
         normed, cotangent, weights, segments[:, None], segments[None, :], q_scale[None, :], k_scale[None, :]
@@ -196,7 +202,7 @@
         normed, cotangent, weights, segment_ids[0, 0], q_gain[0], k_gain[0]
     )
     d_normed = lax.psum_scatter(term, "tensor", scatter_dimension=0, tiled=True)
-    d_outw = contract(attended, cotangent, 0, 0)
+    d_outw = contract(attended, cotangent, 1, 0)
     d_proj = contract(normed, d_joined, 0, 0).astype(jnp.bfloat16)
     gradients = jnp.concatenate(
         [d_proj.reshape(dp, share, three), fold_wide(d_outw.astype(jnp.bfloat16), dp, three)], axis=1

time: 213 us -> 216 us (1.014)
  local copies, waits for them, and re-layouts: 7.11 us -> 13.3 us
  Pallas kernels: 16.9 us -> 13.8 us
    unnamed x18 -> x24, local copies, waits for them, and re-layouts: 5.44 us -> 10.9 us
    pallas_call x1, Pallas kernels: 12.3 us -> 9.22 us  [head_backward(): pl.pallas_call(head_kernel, out_shape=tuple((jax.ShapeDtypeStruct(shape,...]
where the time goes in v5:
time: 216 us; the launch traced here: 215 us
  blocking collectives  120 us (56%)
  waiting for transfers between devices  30.3 us (14%)
  between operations  14.2 us (7%)
  Pallas kernels  13.8 us (6%)
  local copies, waits for them, and re-layouts  13.3 us (6%)
  starting transfers between devices  11.7 us (5%)
  other arithmetic  7.09 us (3%)
  matrix products  4.5 us (2%)
    all_gather x1, blocking collectives, per_device(): blocks = lax.all_gather(block.astype(jnp.float16), 'tensor', axis=0)  82.7 us
    reduce_scatter x1, waiting for transfers between devices, per_device(): d_normed = lax.psum_scatter(term, 'tensor', scatter_dimension=0, tiled=True)  24.8 us
    all_to_all x1, blocking collectives, per_device(): terms = lax.all_to_all(gradients, 'dp', 0, 0)  20.5 us
    all_to_all x1, blocking collectives, per_device(): lax.all_to_all(jnp.broadcast_to(total[None], terms.shape), 'dp', 0, 0)  17.3 us
    ppermute x1, starting transfers between devices, shifted(): lax.ppermute(array, axis, [(i, (i + by) % peers) for i in range(peers)])  11.6 us
    unnamed x24, local copies, waits for them, and re-layouts  10.9 us
    pallas_call x1, Pallas kernels, head_backward(): pl.pallas_call(head_kernel, out_shape=tuple((jax.ShapeDtypeStruct(shape,...  9.22 us
    ppermute x1, waiting for transfers between devices, shifted(): lax.ppermute(array, axis, [(i, (i + by) % peers) for i in range(peers)])  5.51 us
  transfers between devices with their start and end apart: 3, of which 2 were waited for; matrix products, arithmetic and copies ran while one was open for 7% of the time, Pallas kernels for 0%

profile of v5, /device:TPU:1, one launch (start us, length us, event | category | flops | bytes accessed | tf_op | source)
XLA Modules:
  0.0 215.4 jit_solution(16937740107724491234)
XLA Ops:
  7.2 0.0 all-gather.5.cloned.1.call-start
  7.2 2.4 %shard_map.94 = (f32[136,1536]{1,0:T(8,128)}, bf16[256,384]{1,0:T(8,128)(2,1)}) custom-call(bf16[64,1536]{1,0:T(8,128)(2,1)} %bitcast.42, bf16[64,1536]{1,0:T(8,128)(2,1)} %bitcast.44, bf16[192,384]{1,0:T(8,128)(2,1)} %bitcast.55, bf16[16,1536]{1,0:T(8,128)(2,1)} %bitcast.56), custom_call_target="tpu_custom_call" | custom-call | tf_op jit(solution)/shard_map/pallas_call | solution.py:183
  9.6 0.0 all-gather.5.cloned.1.call-update
  9.7 0.0 reduce-scatter.2.cloned.1.call-start
  9.7 1.2 convert_element_type.26
  10.9 82.7 %all-gather.6 = f16[2176,1536]{1,0:T(8,128)(2,1)S(1)} all-gather(f16[136,1536]{1,0:T(8,128)(2,1)S(1)} %convert_element_type.26), channel_id=2, replica_groups=mesh['dp'=8,'pipe'=4,'tensor'=16] {'tensor'}, dimensions={0}, use_global_device_ids=true | all-gather | bytes 7102464 | tf_op jit(solution)/shard_map/all_gather | solution.py:193
  93.6 2.8 %copy-done.8 = f16[2176,1536]{1,0:T(8,128)(2,1)} copy-done((f16[2176,1536]{1,0:T(8,128)(2,1)}, f16[2176,1536]{1,0:T(8,128)(2,1)S(1)}, u32[]{:S(2)}) %copy-start.8) | copy-done | bytes 6684696
  96.4 0.1 slice.62
  96.4 0.4 copy.13
  96.8 0.1 convert_element_type.28
  96.9 1.0 copy.12.seg_col
  97.9 4.8 %multiply_convert_fusion = (bf16[16,64,1536]{2,1,0:T(8,128)(2,1)S(1)}, bf16[16,64,1536]{2,1,0:T(8,128)(2,1)}) fusion(f16[16,136,1536]{2,1,0:T(8,128)(2,1)} %bitcast.39, f32[16]{0:T(128)S(1)} %get-tuple-element.19, f32[16]{0:T(128)S(1)} %get-tuple-element.20), kind=kLoop, calls=%fused_computation | loop fusion | flops 9437184 | bytes 12583040 | tf_op jit(solution)/shard_map/convert_element_type | solution.py:200
  102.8 1.9 copy-done.1
  104.6 1.0 copy-done.2
  105.7 1.4 copy-done.4
  107.1 9.2 %shard_map.95 = (bf16[1024,1536]{1,0:T(8,128)(2,1)S(1)}, bf16[1024,384]{1,0:T(8,128)(2,1)S(1)}, bf16[128,1024]{1,0:T(8,128)(2,1)S(1)}) custom-call(bf16[1024,1536]{1,0:T(8,128)(2,1)S(1)} %bitcast.34, bf16[1024,1536]{1,0:T(8,128)(2,1)S(1)} %bitcast.31, bf16[8,256,384]{2,1,0:T(8,128)(2,1)S(1)} %bitcast.37, s32[1024,1]{1,0:T(8,128)S(1)} %copy-done.2, ...), custom_call_target="tpu_custom_call" | custom-call | flops 5000000000 | bytes 12000000 | tf_op jit(solution)/shard_map/pallas_call | solution.py:154
  116.3 1.6 copy-done
  118.0 0.9 copy-done.7
  118.9 3.9 %convolution_convert_fusion = bf16[1536,384]{1,0:T(8,128)(2,1)S(1)} fusion(bf16[1024,1536]{1,0:T(8,128)(2,1)} %bitcast.33, bf16[1024,384]{1,0:T(8,128)(2,1)} %copy-done.7), kind=kOutput, calls=%fused_computation.2 | convolution fusion | flops 1208549376 | bytes 5111808 | tf_op jit(solution)/shard_map/dot_general | solution.py:21
  122.8 0.1 constant_dynamic-update-slice_fusion.4
  122.9 0.6 convolution_convert_fusion.1
  123.7 20.5 %all_to_all.10 = bf16[8,256,384]{2,1,0:T(8,128)(2,1)S(1)} all-to-all(bf16[8,256,384]{2,1,0:T(8,128)(2,1)S(1)} %constant_dynamic-update-slice_fusion), channel_id=1, replica_groups=mesh['dp'=8,'pipe'=4,'tensor'=16] {'dp'}, dimensions={0} | all-to-all | bytes 3145728 | tf_op jit(solution)/shard_map/all_to_all | solution.py:210
  144.2 0.3 reduce_sum.12
  144.4 0.1 broadcast_in_dim.13
  144.6 17.3 %all_to_all.11 = bf16[8,256,384]{2,1,0:T(8,128)(2,1)S(1)} all-to-all(bf16[8,256,384]{2,1,0:T(8,128)(2,1)S(1)} %broadcast_in_dim.13), channel_id=1, replica_groups=mesh['dp'=8,'pipe'=4,'tensor'=16] {'dp'}, dimensions={0} | all-to-all | bytes 3145728 | tf_op jit(solution)/shard_map/all_to_all | solution.py:212
  161.8 1.1 slice.70
  163.0 24.8 %reduce-scatter.2.cloned.1.call-done.d_normed = bf16[64,1536]{1,0:T(8,128)(2,1)} async-done(((bf16[1024,1536]{1,0:T(8,128)(2,1)}), bf16[64,1536]{1,0:T(8,128)(2,1)}) %reduce-scatter.2.cloned.1.call-update) | async-done | bytes 196624 | tf_op jit(solution)/shard_map/reduce_scatter | solution.py:204
  187.8 2.2 shard_map.96
  190.0 11.6 %collective-permute-start = (bf16[64,1536]{1,0:T(8,128)(2,1)}, bf16[64,1536]{1,0:T(8,128)(2,1)S(1)}, u32[]{:S(2)}, u32[]{:S(2)}) collective-permute-start(bf16[64,1536]{1,0:T(8,128)(2,1)} %shard_map.96), channel_id=1, source_target_pairs={{0,48},{16,0},{32,16},{48,32},{1,49},{17,1},{33,17},{49,33},{2,50}... | collective-permute-start | bytes 589832 | tf_op jit(solution)/shard_map/ppermute | solution.py:17
  201.6 0.8 maximum_bitcast_fusion
  202.4 5.5 %collective-permute-done = bf16[64,1536]{1,0:T(8,128)(2,1)S(1)} collective-permute-done((bf16[64,1536]{1,0:T(8,128)(2,1)}, bf16[64,1536]{1,0:T(8,128)(2,1)S(1)}, u32[]{:S(2)}, u32[]{:S(2)}) %collective-permute-start) | collective-permute-done | bytes 196640 | tf_op jit(solution)/shard_map/ppermute | solution.py:17
  207.9 0.7 copy.19
  (21 shorter events, 0.2 us)
Async XLA Ops:
  7.2 95.6 %all-gather.5.cloned.1.call-start = ((), (), s32[]{:S(2)}) async-start(), calls=%async_computation.4 | async-start | bytes 1769472 | tf_op jit(solution)/shard_map/all_gather | solution.py:192
  9.7 178.1 %reduce-scatter.2.cloned.1.call-start = ((), (), s32[]{:S(2)}) async-start(), calls=%async_computation.3 | async-start | bytes 3342336 | tf_op jit(solution)/shard_map/reduce_scatter | solution.py:204
  93.6 2.8 %copy-start.8 = (f16[2176,1536]{1,0:T(8,128)(2,1)}, f16[2176,1536]{1,0:T(8,128)(2,1)S(1)}, u32[]{:S(2)}) copy-start(f16[2176,1536]{1,0:T(8,128)(2,1)S(1)} %all-gather.6) | copy-start | bytes 20054020
  93.6 3.3 %copy-start.3 = (s32[1,1,1024]{2,1,0:T(1,128)S(1)}, s32[1,1,1024]{2,1,0:T(1,128)}, u32[]{:S(2)}) copy-start(s32[1,1,1024]{2,1,0:T(1,128)} %param.9) | copy-start | bytes 12292
  97.9 4.8 %copy-start.5 = (f32[1,128]{1,0:T(1,128)S(1)}, f32[1,128]{1,0:T(1,128)}, u32[]{:S(2)}) copy-start(f32[1,128]{1,0:T(1,128)} %q_gain.1) | copy-start | bytes 1540
  97.9 4.8 %copy-start.6 = (f32[1,128]{1,0:T(1,128)S(1)}, f32[1,128]{1,0:T(1,128)}, u32[]{:S(2)}) copy-start(f32[1,128]{1,0:T(1,128)} %k_gain.1) | copy-start | bytes 1540
  102.7 1.9 copy-start.1
  104.6 1.0 copy-start.2
  105.7 1.4 copy-start.4
  116.3 1.7 copy-start
  118.0 0.9 copy-start.7
  190.0 17.9 %collective-permute-start = (bf16[64,1536]{1,0:T(8,128)(2,1)}, bf16[64,1536]{1,0:T(8,128)(2,1)S(1)}, u32[]{:S(2)}, u32[]{:S(2)}) collective-permute-start(bf16[64,1536]{1,0:T(8,128)(2,1)} %shard_map.96), channel_id=1, source_target_pairs={{0,48},{16,0},{32,16},{48,32},{1,49},{17,1},{33,17},{49,33},{2,50}... | collective-permute-start | bytes 589832 | tf_op jit(solution)/shard_map/ppermute | solution.py:17
Sparse Core Ops, SparseCore 0:
  10.7 47.3 all-gather.4
  119.0 68.7 reduce-scatter.1

commit v6 on v5

--- a/solution.py
+++ b/solution.py
@@ -67,10 +67,10 @@
 
 
 def head_kernel(
-    normed, cot, weights, seg_col, seg_row, q_gain, k_gain,
-    term, d_joined, attended,
-    proj, outw, made, sems,
-    q_unit, k_unit, q_rate, k_rate, q_norm, k_norm, v_low, d_att, d_key, d_val, k_turned, v_turned,
+    blocks, weights, seg_col, seg_row, q_gain, k_gain,
+    term, d_scaled, attended,
+    proj, outw, made, d_joined, sems,
+    q_unit, k_unit, q_rate, k_rate, q_norm, k_norm, v_low, d_att, d_key, d_val, k_turned, v_turned, x_scale, g_scale,
 ):
     tokens, width = q_norm.shape
     share = proj.shape[0] // weights.shape[0]
@@ -83,9 +83,17 @@
             outw[p * piece : (p + 1) * piece, c * three : (c + 1) * three] = weights[p, low : low + piece, :]
     factor = width ** (-0.5)
     count = tokens // BLOCK
+    each = tokens // blocks.shape[0]
+    features = blocks.shape[2]
     for i in range(count):
         rows = pl.ds(i * BLOCK, BLOCK)
-        joined = jnp.dot(normed[rows, :], proj[...], preferred_element_type=jnp.float32)
+        some = slice(i * BLOCK // each, (i + 1) * BLOCK // each)
+        for at, scale in ((0, x_scale), (features // 2, g_scale)):
+            power = blocks[some, 2 * each : 2 * each + 1, at : at + 1].astype(jnp.float32)
+            scale[rows, :] = jnp.broadcast_to(jnp.exp2(-power), (BLOCK // each, each, 1)).reshape(BLOCK, 1)
+        normed = blocks[some, 0:each, :].reshape(BLOCK, features)
+        cot = blocks[some, each : 2 * each, :].reshape(BLOCK, features)
+        joined = jnp.dot(normed, proj[...], preferred_element_type=jnp.float32) * x_scale[rows, :]
         for at, unit, rate, norm, gain in (
             (0, q_unit, q_rate, q_norm, q_gain),
             (1, k_unit, k_rate, k_norm, k_gain),
@@ -99,7 +107,7 @@
         v_low[rows, :] = joined[:, 2 * width :].astype(jnp.bfloat16)
         v_turned[:, rows] = joined[:, 2 * width :].T.astype(jnp.bfloat16)
         k_turned[:, rows] = (k_unit[rows, :] * k_gain[...]).T.astype(jnp.bfloat16)
-        d_att[rows, :] = contract(cot[rows, :], outw[...], 1, 1).astype(jnp.bfloat16)
+        d_att[rows, :] = (contract(cot, outw[...], 1, 1) * g_scale[rows, :]).astype(jnp.bfloat16)
     d_key[...] = jnp.zeros_like(d_key)
     d_val[...] = jnp.zeros_like(d_val)
     copies = []
@@ -114,9 +122,9 @@
             expd = jnp.where(same, jnp.exp(scores), 0.0)
             probs = expd * (1.0 / jnp.sum(expd, axis=0, keepdims=True))
             probs_low = probs.astype(jnp.bfloat16)
-            attended[:, rows] = jnp.dot(
-                v_turned[:, near], probs_low, preferred_element_type=jnp.float32
-            ).astype(jnp.bfloat16)
+            out = jnp.dot(v_turned[:, near], probs_low, preferred_element_type=jnp.float32).astype(jnp.bfloat16)
+            across = jnp.broadcast_to(g_scale[rows, :], (BLOCK, 8)).T[0:1, :]
+            attended[:, rows] = (out.astype(jnp.float32) * across).astype(jnp.bfloat16)
             d_probs = contract(v_low[near, :], do, 1, 1)
             d_val[near, :] += jnp.dot(probs_low, do, preferred_element_type=jnp.float32)
             delta = jnp.sum(probs * d_probs, axis=0, keepdims=True)
@@ -134,6 +142,7 @@
             d_keys = k_rate[rows, :] * (back - u * jnp.mean(back * u, axis=-1, keepdims=True))
             d_joined[rows, width : 2 * width] = d_keys.astype(jnp.bfloat16)
             d_joined[rows, 2 * width :] = d_val[rows, :].astype(jnp.bfloat16)
+            d_scaled[rows, :] = (d_joined[rows, :].astype(jnp.float32) * x_scale[rows, :]).astype(jnp.bfloat16)
             made[rows, :] = contract(d_joined[rows, :], proj[...], 1, 1).astype(jnp.bfloat16)
             copy = pltpu.make_async_copy(made.at[rows, :], term.at[rows, :], sems.at[i - 1])
             copy.start()
@@ -142,8 +151,8 @@
         copy.wait()
 
 
-def head_backward(normed, cotangent, weights, segments, q_scale, k_scale):
-    tokens, features = normed.shape
+def head_backward(blocks, weights, segments, q_scale, k_scale):
+    tokens, features = segments.shape[0], blocks.shape[2]
     width = q_scale.shape[0]
     here = pl.BlockSpec(memory_space=pltpu.VMEM)
     low = jnp.bfloat16
@@ -156,20 +165,22 @@
         out_shape=tuple(
             jax.ShapeDtypeStruct(shape, low) for shape in ((tokens, features), (tokens, 3 * width), (width, tokens))
         ),
-        in_specs=[here] * 7,
+        in_specs=[here] * 6,
         out_specs=(pl.BlockSpec(memory_space=pl.ANY), here, here),
         scratch_shapes=[
             pltpu.VMEM((features, 3 * width), low), pltpu.VMEM((width, features), low), kept(features, low),
+            kept(3 * width, low),
             pltpu.SemaphoreType.DMA((tokens // BLOCK,)),
             kept(width, jnp.float32), kept(width, jnp.float32), kept(1, jnp.float32), kept(1, jnp.float32),
             kept(width, low), kept(width, low), kept(width, low), kept(width, low),
             kept(width, jnp.float32), kept(width, jnp.float32),
             pltpu.VMEM((width, tokens), low), pltpu.VMEM((width, tokens), low),
+            kept(1, jnp.float32), kept(1, jnp.float32),
         ],
-        compiler_params=pltpu.CompilerParams(vmem_limit_bytes=28 * 1024 * 1024),
+        compiler_params=pltpu.CompilerParams(vmem_limit_bytes=48 * 1024 * 1024),
         cost_estimate=pl.CostEstimate(flops=5_000_000_000, bytes_accessed=12_000_000, transcendentals=1_000_000),
     )(
-        normed, cotangent, weights, segments[:, None], segments[None, :], q_scale[None, :], k_scale[None, :]
+        blocks, weights, segments[:, None], segments[None, :], q_scale[None, :], k_scale[None, :]
     )
 
 
@@ -191,19 +202,12 @@
     )(tokens, cot, w_qkv[0, :, 0, :], w_out[0, 0])
     weights = lax.all_gather(weights, "dp", axis=0)
     blocks = lax.all_gather(block.astype(jnp.float16), "tensor", axis=0)
-    powers = blocks[:, 2 * rows : 2 * rows + 1, :].astype(jnp.float32)
-    halves = (
-        blocks[:, at * rows : (at + 1) * rows].astype(jnp.float32)
-        * jnp.exp2(-powers[:, :, at * features // 2 : at * features // 2 + 1])
-        for at in (0, 1)
-    )
-    normed, cotangent = (half.astype(jnp.bfloat16).reshape(-1, features) for half in halves)
-    term, d_joined, attended = head_backward(
-        normed, cotangent, weights, segment_ids[0, 0], q_gain[0], k_gain[0]
-    )
+    blocks = blocks.astype(jnp.bfloat16)
+    term, d_scaled, attended = head_backward(blocks, weights, segment_ids[0, 0], q_gain[0], k_gain[0])
     d_normed = lax.psum_scatter(term, "tensor", scatter_dimension=0, tiled=True)
+    normed, cotangent = (blocks[:, at : at + rows].reshape(-1, features) for at in (0, rows))
     d_outw = contract(attended, cotangent, 1, 0)
-    d_proj = contract(normed, d_joined, 0, 0).astype(jnp.bfloat16)
+    d_proj = contract(normed, d_scaled, 0, 0).astype(jnp.bfloat16)
     gradients = jnp.concatenate(
         [d_proj.reshape(dp, share, three), fold_wide(d_outw.astype(jnp.bfloat16), dp, three)], axis=1
     )

time: 216 us -> 209 us (0.968)
  local copies, waits for them, and re-layouts: 13.3 us -> 7.21 us
  Pallas kernels: 13.8 us -> 16.8 us
    unnamed x24 -> x13, local copies, waits for them, and re-layouts: 10.9 us -> 2.27 us
    slice x1, local copies, waits for them, and re-layouts: 0.08 us -> 3.34 us  [per_device(): blocks[:, at:at + rows].reshape(-1, features)]
    pallas_call x1, Pallas kernels: 9.22 us -> 12.2 us  [head_backward(): pl.pallas_call(head_kernel, out_shape=tuple((jax.ShapeDtypeStruct(shape,...]
    convert_element_type x2 -> x1, other arithmetic: 4.85 us -> 4.01 us  [per_device(): blocks = blocks.astype(jnp.bfloat16)]
where the time goes in v6:
time: 209 us; the launch traced here: 208 us
  blocking collectives  120 us (57%)
  waiting for transfers between devices  29.1 us (14%)
  Pallas kernels  16.8 us (8%)
  between operations  14.2 us (7%)
  starting transfers between devices  11.8 us (6%)
  local copies, waits for them, and re-layouts  7.21 us (3%)
  other arithmetic  6.24 us (3%)
  matrix products  2.42 us (1%)
    all_gather x1, blocking collectives, per_device(): blocks = lax.all_gather(block.astype(jnp.float16), 'tensor', axis=0)  82.7 us
    reduce_scatter x1, waiting for transfers between devices, per_device(): d_normed = lax.psum_scatter(term, 'tensor', scatter_dimension=0, tiled=True)  23.6 us
    all_to_all x1, blocking collectives, per_device(): terms = lax.all_to_all(gradients, 'dp', 0, 0)  20.5 us
    all_to_all x1, blocking collectives, per_device(): lax.all_to_all(jnp.broadcast_to(total[None], terms.shape), 'dp', 0, 0)  17.3 us
    pallas_call x1, Pallas kernels, head_backward(): pl.pallas_call(head_kernel, out_shape=tuple((jax.ShapeDtypeStruct(shape,...  12.2 us
    ppermute x1, starting transfers between devices, shifted(): lax.ppermute(array, axis, [(i, (i + by) % peers) for i in range(peers)])  11.7 us
    ppermute x1, waiting for transfers between devices, shifted(): lax.ppermute(array, axis, [(i, (i + by) % peers) for i in range(peers)])  5.45 us
  transfers between devices with their start and end apart: 3, of which 2 were waited for; matrix products, arithmetic and copies ran while one was open for 7% of the time, Pallas kernels for 0%

profile of v6, /device:TPU:1, one launch (start us, length us, event | category | flops | bytes accessed | tf_op | source)
XLA Modules:
  0.0 208.2 jit_solution(341999259635751626)
XLA Ops:
  7.2 0.0 all-gather.5.cloned.1.call-start
  7.2 2.4 %shard_map.94 = (f32[136,1536]{1,0:T(8,128)}, bf16[256,384]{1,0:T(8,128)(2,1)}) custom-call(bf16[64,1536]{1,0:T(8,128)(2,1)} %bitcast.36, bf16[64,1536]{1,0:T(8,128)(2,1)} %bitcast.38, bf16[192,384]{1,0:T(8,128)(2,1)} %bitcast.49, bf16[16,1536]{1,0:T(8,128)(2,1)} %bitcast.50), custom_call_target="tpu_custom_call" | custom-call | tf_op jit(solution)/shard_map/pallas_call | solution.py:194
  9.6 0.0 all-gather.5.cloned.1.call-update
  9.7 0.0 reduce-scatter.2.cloned.1.call-start
  9.7 1.2 convert_element_type.14
  10.9 82.7 %all-gather.6 = f16[2176,1536]{1,0:T(8,128)(2,1)S(1)} all-gather(f16[136,1536]{1,0:T(8,128)(2,1)S(1)} %convert_element_type.14), channel_id=2, replica_groups=mesh['dp'=8,'pipe'=4,'tensor'=16] {'tensor'}, dimensions={0}, use_global_device_ids=true | all-gather | bytes 7102464 | tf_op jit(solution)/shard_map/all_gather | solution.py:204
  93.6 0.0 copy-start
  93.6 4.0 %convert_element_type.18 = bf16[2176,1536]{1,0:T(8,128)(2,1)} convert(f16[2176,1536]{1,0:T(8,128)(2,1)S(1)} %all-gather.6) | non-fusion elementwise | flops 3342336 | bytes 13369344 | tf_op jit(solution)/shard_map/convert_element_type | solution.py:205
  97.6 0.0 copy-done
  97.6 0.2 copy.10.seg_col
  97.8 0.0 all-gather.5.cloned.1.call-done
  97.9 0.0 copy-done.2
  97.9 0.0 copy-done.3
  97.9 0.0 copy-start.1
  97.9 1.4 copy-done.1
  99.3 12.2 %shard_map.95 = (bf16[1024,1536]{1,0:T(8,128)(2,1)}, bf16[1024,384]{1,0:T(8,128)(2,1)S(1)}, bf16[128,1024]{1,0:T(8,128)(2,1)S(1)}) custom-call(bf16[16,136,1536]{2,1,0:T(8,128)(2,1)} %bitcast.30, bf16[8,256,384]{2,1,0:T(8,128)(2,1)S(1)} %bitcast.29, s32[1024,1]{1,0:T(8,128)S(1)} %copy.10.seg_col, s32[1,1024]{1,0:T(1,128)S(1)} %bitcast.28, ...), custom_call_target="tpu_custom_call" | custom-call | flops 5000000000 | bytes 12000000 | tf_op jit(solution)/shard_map/pallas_call | solution.py:163
  111.5 0.0 reduce-scatter.2.cloned.1.call-update
  111.6 3.3 %fusion = (bf16[16,64,1536]{2,1,0:T(8,128)(2,1)S(1)}, bf16[16,64,1536]{2,1,0:T(8,128)(2,1)S(1)}) fusion(bf16[16,136,1536]{2,1,0:T(8,128)(2,1)} %bitcast.31), kind=kLoop, calls=%fused_computation.8 | loop fusion | bytes 12582912 | tf_op jit(solution)/shard_map/slice | solution.py:208
  114.9 1.8 convolution_convert_fusion
  116.8 0.1 constant_dynamic-update-slice_fusion.4
  116.9 0.6 convolution_convert_fusion.1
  117.6 20.5 %all_to_all.10 = bf16[8,256,384]{2,1,0:T(8,128)(2,1)S(1)} all-to-all(bf16[8,256,384]{2,1,0:T(8,128)(2,1)S(1)} %constant_dynamic-update-slice_fusion), channel_id=1, replica_groups=mesh['dp'=8,'pipe'=4,'tensor'=16] {'dp'}, dimensions={0} | all-to-all | bytes 3145728 | tf_op jit(solution)/shard_map/all_to_all | solution.py:214
  138.1 0.3 reduce_sum.12
  138.4 0.1 broadcast_in_dim.13
  138.5 17.3 %all_to_all.11 = bf16[8,256,384]{2,1,0:T(8,128)(2,1)S(1)} all-to-all(bf16[8,256,384]{2,1,0:T(8,128)(2,1)S(1)} %broadcast_in_dim.13), channel_id=1, replica_groups=mesh['dp'=8,'pipe'=4,'tensor'=16] {'dp'}, dimensions={0} | all-to-all | bytes 3145728 | tf_op jit(solution)/shard_map/all_to_all | solution.py:216
  155.8 1.1 slice.55
  157.0 23.6 %reduce-scatter.2.cloned.1.call-done.d_normed = bf16[64,1536]{1,0:T(8,128)(2,1)} async-done(((bf16[1024,1536]{1,0:T(8,128)(2,1)}), bf16[64,1536]{1,0:T(8,128)(2,1)}) %reduce-scatter.2.cloned.1.call-update) | async-done | bytes 196624 | tf_op jit(solution)/shard_map/reduce_scatter | solution.py:207
  180.6 2.2 %shard_map.96 = bf16[64,1536]{1,0:T(8,128)(2,1)} custom-call(bf16[64,1536]{1,0:T(8,128)(2,1)} %bitcast.37, bf16[64,1536]{1,0:T(8,128)(2,1)} %bitcast.39, bf16[64,1536]{1,0:T(8,128)(2,1)} %reduce-scatter.2.cloned.1.call-done.d_normed), custom_call_target="tpu_custom_call" | custom-call | tf_op jit(solution)/shard_map/pallas_call | solution.py:219
  182.7 11.7 %collective-permute-start = (bf16[64,1536]{1,0:T(8,128)(2,1)}, bf16[64,1536]{1,0:T(8,128)(2,1)S(1)}, u32[]{:S(2)}, u32[]{:S(2)}) collective-permute-start(bf16[64,1536]{1,0:T(8,128)(2,1)} %shard_map.96), channel_id=1, source_target_pairs={{0,48},{16,0},{32,16},{48,32},{1,49},{17,1},{33,17},{49,33},{2,50}... | collective-permute-start | bytes 589832 | tf_op jit(solution)/shard_map/ppermute | solution.py:17
  194.5 0.8 maximum_bitcast_fusion
  195.2 5.5 %collective-permute-done = bf16[64,1536]{1,0:T(8,128)(2,1)S(1)} collective-permute-done((bf16[64,1536]{1,0:T(8,128)(2,1)}, bf16[64,1536]{1,0:T(8,128)(2,1)S(1)}, u32[]{:S(2)}, u32[]{:S(2)}) %collective-permute-start) | collective-permute-done | bytes 196640 | tf_op jit(solution)/shard_map/ppermute | solution.py:17
  200.7 0.7 copy.16
  (8 shorter events, 0.2 us)
Async XLA Ops:
  7.2 90.7 %all-gather.5.cloned.1.call-start = ((), (), s32[]{:S(2)}) async-start(), calls=%async_computation.4 | async-start | bytes 1769472 | tf_op jit(solution)/shard_map/all_gather | solution.py:203
  9.7 170.9 %reduce-scatter.2.cloned.1.call-start = ((), (), s32[]{:S(2)}) async-start(), calls=%async_computation.3 | async-start | bytes 3342336 | tf_op jit(solution)/shard_map/reduce_scatter | solution.py:207
  93.6 4.0 %copy-start = (s32[1,1,1024]{2,1,0:T(1,128)S(1)}, s32[1,1,1024]{2,1,0:T(1,128)}, u32[]{:S(2)}) copy-start(s32[1,1,1024]{2,1,0:T(1,128)} %param.9) | copy-start | bytes 12292
  93.6 4.3 %copy-start.2 = (f32[1,128]{1,0:T(1,128)S(1)}, f32[1,128]{1,0:T(1,128)}, u32[]{:S(2)}) copy-start(f32[1,128]{1,0:T(1,128)} %q_gain.1) | copy-start | bytes 1540
  93.6 4.3 %copy-start.3 = (f32[1,128]{1,0:T(1,128)S(1)}, f32[1,128]{1,0:T(1,128)}, u32[]{:S(2)}) copy-start(f32[1,128]{1,0:T(1,128)} %k_gain.1) | copy-start | bytes 1540
  97.9 1.4 copy-start.1
  182.7 18.0 %collective-permute-start = (bf16[64,1536]{1,0:T(8,128)(2,1)}, bf16[64,1536]{1,0:T(8,128)(2,1)S(1)}, u32[]{:S(2)}, u32[]{:S(2)}) collective-permute-start(bf16[64,1536]{1,0:T(8,128)(2,1)} %shard_map.96), channel_id=1, source_target_pairs={{0,48},{16,0},{32,16},{48,32},{1,49},{17,1},{33,17},{49,33},{2,50}... | collective-permute-start | bytes 589832 | tf_op jit(solution)/shard_map/ppermute | solution.py:17
Sparse Core Ops, SparseCore 0:
  10.7 47.3 all-gather.4
  111.7 68.8 reduce-scatter.1
